TPU v7x, 32 devices: a whole 2x2x4 slice. The times are simulated.
32 devices in a mesh: slot: 8 (over z, y), hid: 4 (over x, core).
Axes of the slice: x: 2, y: 2, z: 4, core: 2. Of those that a mesh axis runs over, the one named last changes fastest.
Arguments:
- master: float32 [4, 3, 4, 393216], P(None, None, 'hid', 'slot'), may hold values from -0.125 to 0.125
- first_moment: float32 [4, 3, 4, 393216], P(None, None, 'hid', 'slot'), may hold values from -0.3 to 0.3
- second_moment: float32 [4, 3, 4, 393216], P(None, None, 'hid', 'slot'), may hold values from 0.0001 to 0.01
- slot_weights: bfloat16 [8, 3, 768, 2048], P('slot', None, 'hid'), may hold values from -0.125 to 0.125
- back_rows: bfloat16 [8, 1024, 2048], P('slot'), may hold values from -6 to 6
- readout: bfloat16 [8, 1024, 2048], P('slot'), may hold values from -0.25 to 0.25
- ref_logratio: float32 [8, 1024], P('slot'), may hold values from -9 to 0
- labels: int32 [8, 1024], P('slot'), may hold values 0 or 1
- place_cur: int32 [8], replicated, may hold values from 0 to 3, as said below
- place_next: int32 [8], replicated, may hold values from 0 to 3, as said below
- fwd_rows: bfloat16 [2048, 2048], P('slot', 'hid'), may hold values from -6 to 6
- routes: int32 [2048, 1], P('slot'), may hold values from 0 to 7; in each aligned block of 256 rows (0 to 255, 256 to 511, ...) at most 64 rows name the same one
Outputs:
- out_rows: bfloat16 [2048, 2048], P('slot', 'hid')
- new_master: float32 [4, 3, 4, 393216], P(None, None, 'hid', 'slot')
- new_first: float32 [4, 3, 4, 393216], P(None, None, 'hid', 'slot')
- new_second: float32 [4, 3, 4, 393216], P(None, None, 'hid', 'slot')
Inputs may be any that keep to these rules, and one draw needn't show every extreme that they name: `place_cur`: every expert 0 to 3 is held by at least one slot. `place_next`: every expert 0 to 3 is held by at least one slot. `routes`: the rows of one slot name any one slot at most 64 times, a bound that some block reaches.
All inputs are finite; a program needn't handle non-finite values. No bound on the sum of `labels` on one device may be relied on, other than what follows from the above.
Results may differ from a plain program's by a relative error of at most 0.008.
Values may be sent and summed in bfloat16 or wider, within the bound.
A program may use at most 128 MiB of HBM per device.

v0:
```python
import jax
import jax.numpy as jnp
from jax import lax
from jax.sharding import PartitionSpec as P

beta_kto = 1.0
desired_weight = 1.0
undesired_weight = 1.33
learn_rate = 0.004
decay_first = 0.9
decay_second = 0.999
correct_first = 0.9999734386011124
correct_second = 0.09520785288629043
adam_eps = 1e-08
weight_decay = 0.1


def expert_pass(inputs, weights):
    across = (((1,), (1,)), ((), ()))
    gate_vals = lax.dot_general(inputs, weights[0], across, preferred_element_type=jnp.float32)
    up_vals = lax.dot_general(inputs, weights[1], across, preferred_element_type=jnp.float32)
    hidden = (gate_vals * jax.nn.sigmoid(gate_vals) * up_vals).astype(jnp.bfloat16)
    produced = jnp.dot(hidden, weights[2], preferred_element_type=jnp.float32)
    return (gate_vals, up_vals, hidden, produced)


def kto_slope(scores, labels, center):
    sigma_v = jax.nn.sigmoid(beta_kto * (scores - center))
    signed = jnp.where(labels == 1, -desired_weight, undesired_weight)
    return beta_kto * sigma_v * (1.0 - sigma_v) * signed


def expert_backward(inputs, direction, weights, slope, gate_vals, up_vals, hidden):
    d_expert = (slope[:, None] * direction.astype(jnp.float32)).astype(jnp.bfloat16)
    d_hidden = lax.dot_general(
        d_expert, weights[2], (((1,), (1,)), ((), ())), preferred_element_type=jnp.float32
    )
    sigma_g = jax.nn.sigmoid(gate_vals)
    d_gate = (d_hidden * up_vals * sigma_g * (1.0 + gate_vals * (1.0 - sigma_g))).astype(
        jnp.bfloat16
    )
    d_up = (d_hidden * gate_vals * sigma_g).astype(jnp.bfloat16)
    contract = (((0,), (0,)), ((), ()))
    grad_gate = lax.dot_general(d_gate, inputs, contract, preferred_element_type=jnp.float32)
    grad_up = lax.dot_general(d_up, inputs, contract, preferred_element_type=jnp.float32)
    grad_down = lax.dot_general(hidden, d_expert, contract, preferred_element_type=jnp.float32)
    return jnp.stack([grad_gate, grad_up, grad_down])


def adamw_update(master, first_moment, second_moment, summed):
    new_first = decay_first * first_moment + (1.0 - decay_first) * summed
    new_second = decay_second * second_moment + (1.0 - decay_second) * summed * summed
    update = new_first / correct_first / (jnp.sqrt(new_second / correct_second) + adam_eps)
    new_master = master - learn_rate * (update + weight_decay * master)
    return (new_master, new_first, new_second)


def shards(
    master,
    first_moment,
    second_moment,
    slot_weights,
    back_rows,
    readout,
    ref_logratio,
    labels,
    place_cur,
    place_next,
    fwd_rows,
    routes,
):
    slot_count = lax.axis_size("slot")
    experts_here = master.shape[0]
    weights = slot_weights[0]
    width = weights.shape[2]
    owned_units = master.shape[3] // width
    inputs = back_rows[0]
    direction = readout[0]
    gate_vals, up_vals, hidden, partial_value = expert_pass(inputs, weights)
    row_part = jnp.sum(partial_value * direction.astype(jnp.float32), axis=1)
    policy = lax.psum(row_part, "hid")
    scores = policy - ref_logratio[0]
    row_total = slot_count * inputs.shape[0]
    center = lax.psum(jnp.sum(scores), "slot") / row_total
    slope = kto_slope(scores, labels[0], center)
    grads = expert_backward(inputs, direction, weights, slope, gate_vals, up_vals, hidden)
    arrived = lax.all_to_all(
        grads[None].astype(jnp.bfloat16), "slot", split_axis=2, concat_axis=0, tiled=True
    ).astype(jnp.float32)
    arrived = arrived.reshape(slot_count, 3, 1, owned_units * width)
    owner_map = (place_cur[None, :] == jnp.arange(experts_here, dtype=jnp.int32)[:, None]).astype(
        jnp.float32
    )
    summed = jnp.einsum("es,sabc->eabc", owner_map, arrived, precision=lax.Precision.HIGHEST)
    new_master, new_first, new_second = adamw_update(master, first_moment, second_moment, summed)
    refreshed = new_master.astype(jnp.bfloat16)
    pick_map = (place_next[:, None] == jnp.arange(experts_here, dtype=jnp.int32)[None, :]).astype(
        jnp.bfloat16
    )
    picked = jnp.einsum(
        "se,eabc->sabc", pick_map, refreshed, preferred_element_type=jnp.float32
    ).astype(jnp.bfloat16)
    picked = picked.reshape(slot_count, 3, owned_units, width)
    resident = lax.all_to_all(picked, "slot", split_axis=0, concat_axis=2, tiled=True)[0]
    capacity = 2 * fwd_rows.shape[0] // slot_count
    quarter = fwd_rows.shape[1]
    target = routes[:, 0]
    target_map = (target[:, None] == jnp.arange(slot_count, dtype=jnp.int32)[None, :]).astype(
        jnp.int32
    )
    earlier = jnp.cumsum(target_map, axis=0) - target_map
    position = jnp.sum(earlier * target_map, axis=1)
    slot_place = target * capacity + position
    place_map = (
        slot_place[None, :] == jnp.arange(slot_count * capacity, dtype=jnp.int32)[:, None]
    ).astype(jnp.bfloat16)
    buffer_rows = jnp.dot(place_map, fwd_rows, preferred_element_type=jnp.float32).astype(
        jnp.bfloat16
    )
    buffer_rows = buffer_rows.reshape(slot_count, capacity, quarter)
    arrived_rows = lax.all_to_all(
        buffer_rows, "slot", split_axis=0, concat_axis=0, tiled=True
    ).reshape(slot_count * capacity, quarter)
    across = (((1,), (1,)), ((), ()))
    piece_rows = lax.all_gather(arrived_rows, "hid", axis=1, tiled=True)
    gate_cols = resident[0]
    up_cols = resident[1]
    fwd_gate = lax.dot_general(piece_rows, gate_cols, across, preferred_element_type=jnp.float32)
    fwd_up = lax.dot_general(piece_rows, up_cols, across, preferred_element_type=jnp.float32)
    fwd_hidden = (fwd_gate * jax.nn.sigmoid(fwd_gate) * fwd_up).astype(jnp.bfloat16)
    fwd_partial = jnp.dot(fwd_hidden, resident[2], preferred_element_type=jnp.float32)
    totals = lax.psum(fwd_partial, "hid")
    shares = lax.dynamic_slice_in_dim(totals, lax.axis_index("hid") * quarter, quarter, 1)
    outgoing = shares.astype(jnp.bfloat16).reshape(slot_count, capacity, quarter)
    returned = lax.all_to_all(outgoing, "slot", split_axis=0, concat_axis=0, tiled=True).reshape(
        slot_count * capacity, quarter
    )
    out_rows = lax.dot_general(
        place_map, returned, (((0,), (0,)), ((), ())), preferred_element_type=jnp.float32
    ).astype(jnp.bfloat16)
    return (out_rows, new_master, new_first, new_second)


def solution(mesh):
    return jax.shard_map(
        shards,
        mesh=mesh,
        in_specs=(
            P(None, None, "hid", "slot"),
            P(None, None, "hid", "slot"),
            P(None, None, "hid", "slot"),
            P("slot", None, "hid", None),
            P("slot", None, None),
            P("slot", None, None),
            P("slot", None),
            P("slot", None),
            P(),
            P(),
            P("slot", "hid"),
            P("slot", None),
        ),
        out_specs=(
            P("slot", "hid"),
            P(None, None, "hid", "slot"),
            P(None, None, "hid", "slot"),
            P(None, None, "hid", "slot"),
        ),
        check_vma=False,
    )
```

profile of v0, /device:TPU:1, one launch (start us, length us, event | category | flops | bytes accessed | tf_op | source)
XLA Modules:
  0.0 325.8 jit_solution(14636702760616100537)
XLA Ops:
  7.2 4.1 %fusion.16 = f32[1024,192]{0,1:T(8,128)S(1)} fusion(bf16[1,1024,2048]{2,1,0:T(8,128)(2,1)} %param.16, bf16[1,3,192,2048]{3,2,1,0:T(8,128)(2,1)} %param.15), kind=kOutput, calls=%fused_computation.17 | convolution fusion | flops 805306368 | bytes 5767168 | tf_op jit(solution)/shard_map/dot_general | solution.py:20
  11.6 2.5 multiply_convert_fusion.2
  14.8 1.4 fusion.2
  16.3 6.4 %psum.21 = f32[1024]{0:T(1024)S(1)} all-reduce(f32[1024]{0:T(1024)S(1)} %fusion.2), channel_id=1, replica_groups=mesh['slot'=8,'hid'=4] {'hid'}, use_global_device_ids=true, to_apply=%region_4.5 | all-reduce | flops 1024 | bytes 8192 | tf_op jit(solution)/shard_map/psum | solution.py:81
  23.3 18.7 %psum.22 = f32[]{:T(128)} all-reduce(f32[]{:T(128)} %get-tuple-element.19), channel_id=1, replica_groups=mesh['slot'=8,'hid'=4] {'slot'}, use_global_device_ids=true, to_apply=%region_6.7 | all-reduce | flops 1 | bytes 8 | tf_op jit(solution)/shard_map/psum | solution.py:84
  42.6 3.9 %fusion.6 = f32[1024,192]{0,1:T(8,128)S(1)} fusion(bf16[1,1024,2048]{2,1,0:T(8,128)(2,1)} %param.17, f32[1024]{0:T(1024)S(1)} %fusion.65, bf16[1,3,192,2048]{3,2,1,0:T(8,128)(2,1)S(1)} %copy-done.12), kind=kOutput, calls=%fused_computation.9 | convolution fusion | flops 811597824 | bytes 5771264 | tf_op jit(solution)/shard_map/dot_general | solution.py:35
  46.6 1.1 fusion.35
  48.8 1.1 fusion.29
  49.9 1.2 fusion.32
  51.4 3.7 %copy.32 = bf16[1,3,192,2048]{3,1,0,2:T(4,128)(2,1)} copy(bf16[1,3,192,2048]{3,2,1,0:T(8,128)(2,1)S(1)} %pad_maximum_fusion) | data formatting | bytes 4718592 | tf_op jit(solution)/shard_map/stack | solution.py:47
  55.1 3.8 %all-to-all-start.1 = ((bf16[1,3,192,2048]{3,1,0,2:T(4,128)(2,1)}), bf16[1,3,192,2048]{3,1,0,2:T(4,128)(2,1)S(1)}, u32[]{:S(2)}, u32[]{:S(2)}) async-start(bf16[1,3,192,2048]{3,1,0,2:T(4,128)(2,1)} %copy.32), calls=%async_computation.1 | async-start | bytes 6291456 | tf_op jit(solution)/shard_map/all_to_all | solution.py:87
  59.8 1.1 convolution_convert_fusion.1
  61.0 63.7 %all-to-all-done.1 = bf16[1,3,192,2048]{3,1,0,2:T(4,128)(2,1)S(1)} async-done(((bf16[1,3,192,2048]{3,1,0,2:T(4,128)(2,1)}), bf16[1,3,192,2048]{3,1,0,2:T(4,128)(2,1)S(1)}, u32[]{:S(2)}, u32[]{:S(2)}) %all-to-all-start.1) | async-done | bytes 2359328 | tf_op jit(solution)/shard_map/all_to_all | solution.py:87
  124.7 8.6 %all-to-all-start = ((bf16[8,64,512]{2,1,0:T(8,128)(2,1)}), bf16[8,64,512]{2,1,0:T(8,128)(2,1)}, u32[]{:S(2)}, u32[]{:S(2)}) async-start(bf16[8,64,512]{2,1,0:T(8,128)(2,1)} %bitcast.120), calls=%async_computation | async-start | bytes 1048576 | tf_op jit(solution)/shard_map/all_to_all | solution.py:121
  133.3 1.7 copy.33
  135.7 9.7 %multiply_subtract_fusion = (f32[4,3,1,49152]{3,0,1,2:T(4,128)S(1)}, f32[4,3,1,49152]{3,0,1,2:T(4,128)}, f32[4,3,1,49152]{3,0,1,2:T(4,128)}) fusion(f32[4,3,1,49152]{3,2,1,0:T(1,128)S(1)} %copy-done.13, f32[4,3,1,49152]{3,2,1,0:T(1,128)S(1)} %copy-done.14, f32[4,3,1,49152]{3,2,1,0:T(1,128)} %param.14, bf16[8,3,49152]{2,0,1:T(8,128)(2,1)S(1)} %bitcast.119, ...), kind=kOutput, calls=%fused_computation.35 | convolution fusion | flops 18284576 | bytes 16515104 | tf_op jit(solution)/shard_map/es,sabc->eabc/dot_general | solution.py:94
  145.4 1.1 convolution_convert_fusion
  146.5 2.7 copy.37
  149.2 5.4 %all-to-all-start.2 = ((bf16[8,3,24,2048]{3,2,1,0:T(8,128)(2,1)}), bf16[8,3,24,2048]{3,2,1,0:T(8,128)(2,1)}, u32[]{:S(2)}, u32[]{:S(2)}) async-start(bf16[8,3,24,2048]{3,2,1,0:T(8,128)(2,1)} %copy.37), calls=%async_computation.2 | async-start | bytes 4718592 | tf_op jit(solution)/shard_map/all_to_all | solution.py:104
  155.4 51.3 %all-to-all-done.2 = bf16[8,3,24,2048]{3,2,1,0:T(8,128)(2,1)} async-done(((bf16[8,3,24,2048]{3,2,1,0:T(8,128)(2,1)}), bf16[8,3,24,2048]{3,2,1,0:T(8,128)(2,1)}, u32[]{:S(2)}, u32[]{:S(2)}) %all-to-all-start.2) | async-done | bytes 2359328 | tf_op jit(solution)/shard_map/all_to_all | solution.py:104
  206.7 1.8 copy.52
  208.6 1.3 fusion.78
  209.9 3.4 %fusion.79 = f32[512,192]{0,1:T(8,128)} fusion(bf16[512,2048]{1,0:T(8,128)(2,1)} %all-gather.2.cloned.1.call-done, bf16[192,2048]{1,0:T(8,128)(2,1)} %bitcast.121), kind=kOutput, calls=%fused_computation.90 | convolution fusion | flops 402653184 | bytes 3276800 | tf_op jit(solution)/shard_map/dot_general | solution.py:128
  213.3 5.4 %fusion.43 = f32[512,2048]{1,0:T(8,128)} fusion(bf16[192,2048]{1,0:T(8,128)(2,1)S(1)} %bitcast.117, bf16[512,2048]{1,0:T(8,128)(2,1)} %all-gather.2.cloned.1.call-done, bf16[192,2048]{1,0:T(8,128)(2,1)} %bitcast.118, f32[512,192]{0,1:T(8,128)} %fusion.79), kind=kOutput, calls=%fused_computation.42 | convolution fusion | flops 805896192 | bytes 8257536 | tf_op jit(solution)/shard_map/dot_general | solution.py:131
  218.7 78.6 %all-reduce.1 = bf16[512,2048]{1,0:T(8,128)(2,1)} all-reduce(f32[512,2048]{1,0:T(8,128)} %fusion.43), channel_id=1, replica_groups=mesh['slot'=8,'hid'=4] {'hid'}, use_global_device_ids=true, to_apply=%region_7.8 | all-reduce | flops 1048576 | bytes 6291456 | tf_op jit(solution)/shard_map/psum | solution.py:132
  297.3 1.9 dynamic-slice_convert_fusion
  299.1 4.9 %all-to-all-start.3 = ((bf16[8,64,512]{2,1,0:T(8,128)(2,1)}), bf16[8,64,512]{2,1,0:T(8,128)(2,1)S(1)}, u32[]{:S(2)}, u32[]{:S(2)}) async-start(bf16[8,64,512]{2,1,0:T(8,128)(2,1)} %bitcast.32), calls=%async_computation.3 | async-start | bytes 1048576 | tf_op jit(solution)/shard_map/all_to_all | solution.py:135
  304.0 3.8 %copy.39 = f32[4,3,1,49152]{3,2,1,0:T(1,128)} copy(f32[4,3,1,49152]{3,0,1,2:T(4,128)S(1)} %get-tuple-element.16) | data formatting | bytes 4718592
  307.9 3.8 %copy.40 = f32[4,3,1,49152]{3,2,1,0:T(1,128)} copy(f32[4,3,1,49152]{3,0,1,2:T(4,128)S(1)} %copy-done.3) | data formatting | bytes 4718592
  311.7 3.8 %copy.41 = f32[4,3,1,49152]{3,2,1,0:T(1,128)} copy(f32[4,3,1,49152]{3,0,1,2:T(4,128)S(1)} %copy-done.2) | data formatting | bytes 4718592
  315.5 2.4 all-to-all-done.3
  317.9 1.1 convolution_convert_fusion.2
  (53 shorter events, 5.4 us)
Async XLA Ops:
  7.2 52.7 %copy-start = (bf16[256,512]{1,0:T(8,128)(2,1)S(1)}, bf16[256,512]{1,0:T(8,128)(2,1)}, u32[]{:S(2)}) copy-start(bf16[256,512]{1,0:T(8,128)(2,1)} %param.22) | copy-start | bytes 786436
  7.2 4.1 %copy-start.12 = (bf16[1,3,192,2048]{3,2,1,0:T(8,128)(2,1)S(1)}, bf16[1,3,192,2048]{3,2,1,0:T(8,128)(2,1)}, u32[]{:S(2)}) copy-start(bf16[1,3,192,2048]{3,2,1,0:T(8,128)(2,1)} %param.15) | copy-start | bytes 7077892
  7.2 4.4 %copy-start.10 = (bf16[1,1024,2048]{2,1,0:T(8,128)(2,1)S(1)}, bf16[1,1024,2048]{2,1,0:T(8,128)(2,1)}, u32[]{:S(2)}) copy-start(bf16[1,1024,2048]{2,1,0:T(8,128)(2,1)} %param.16) | copy-start | bytes 12582916
  11.6 3.2 copy-start.8
  14.1 0.7 copy-start.17
  14.8 7.8 %copy-start.5 = (f32[1,1024]{1,0:T(1,128)S(1)}, f32[1,1024]{1,0:T(1,128)}, u32[]{:S(2)}) copy-start(f32[1,1024]{1,0:T(1,128)} %param.18) | copy-start | bytes 12292
  14.8 27.1 %copy-start.6 = (s32[1,1024]{1,0:T(1,128)S(1)}, s32[1,1024]{1,0:T(1,128)}, u32[]{:S(2)}) copy-start(s32[1,1024]{1,0:T(1,128)} %param.19) | copy-start | bytes 12292
  42.6 4.0 %copy-start.9 = (bf16[1,1024,2048]{2,1,0:T(8,128)(2,1)S(1)}, bf16[1,1024,2048]{2,1,0:T(8,128)(2,1)}, u32[]{:S(2)}) copy-start(bf16[1,1024,2048]{2,1,0:T(8,128)(2,1)} %param.17) | copy-start | bytes 12582916
  42.6 4.0 %copy-start.18 = (bf16[1024,192]{0,1:T(8,128)(2,1)S(1)}, bf16[1024,192]{0,1:T(8,128)(2,1)}, u32[]{:S(2)}) copy-start(bf16[1024,192]{0,1:T(8,128)(2,1)} %copy-done.17) | copy-start | bytes 1179652
  46.6 2.2 copy-start.11
  48.8 1.1 copy-start.16
  55.1 3.8 %copy-start.4 = (s32[256,1]{0,1:T(1,128)S(1)}, s32[256,1]{0,1:T(1,128)}, u32[]{:S(2)}) copy-start(s32[256,1]{0,1:T(1,128)} %param.23) | copy-start | bytes 3076
  55.1 69.6 %all-to-all-start.1 = ((bf16[1,3,192,2048]{3,1,0,2:T(4,128)(2,1)}), bf16[1,3,192,2048]{3,1,0,2:T(4,128)(2,1)S(1)}, u32[]{:S(2)}, u32[]{:S(2)}) async-start(bf16[1,3,192,2048]{3,1,0,2:T(4,128)(2,1)} %copy.32), calls=%async_computation.1 | async-start | bytes 6291456 | tf_op jit(solution)/shard_map/all_to_all | solution.py:87
  124.7 24.5 %all-to-all-start = ((bf16[8,64,512]{2,1,0:T(8,128)(2,1)}), bf16[8,64,512]{2,1,0:T(8,128)(2,1)}, u32[]{:S(2)}, u32[]{:S(2)}) async-start(bf16[8,64,512]{2,1,0:T(8,128)(2,1)} %bitcast.120), calls=%async_computation | async-start | bytes 1048576 | tf_op jit(solution)/shard_map/all_to_all | solution.py:121
  133.3 1.7 copy-start.13
  133.3 2.4 copy-start.14
  133.3 2.4 copy-start.15
  135.7 9.7 %copy-start.7 = (s32[8]{0:T(128)S(1)}, s32[8]{0:T(128)}, u32[]{:S(2)}) copy-start(s32[8]{0:T(128)} %param.21) | copy-start | bytes 100
  149.2 57.5 %all-to-all-start.2 = ((bf16[8,3,24,2048]{3,2,1,0:T(8,128)(2,1)}), bf16[8,3,24,2048]{3,2,1,0:T(8,128)(2,1)}, u32[]{:S(2)}, u32[]{:S(2)}) async-start(bf16[8,3,24,2048]{3,2,1,0:T(8,128)(2,1)} %copy.37), calls=%async_computation.2 | async-start | bytes 4718592 | tf_op jit(solution)/shard_map/all_to_all | solution.py:104
  154.7 55.2 %all-gather.2.cloned.1.call-start = ((), (), s32[]{:S(2)}) async-start(), calls=%async_computation.4 | async-start | bytes 2621440 | tf_op jit(solution)/shard_map/all_gather | solution.py:125
  299.1 18.8 %all-to-all-start.3 = ((bf16[8,64,512]{2,1,0:T(8,128)(2,1)}), bf16[8,64,512]{2,1,0:T(8,128)(2,1)S(1)}, u32[]{:S(2)}, u32[]{:S(2)}) async-start(bf16[8,64,512]{2,1,0:T(8,128)(2,1)} %bitcast.32), calls=%async_computation.3 | async-start | bytes 1048576 | tf_op jit(solution)/shard_map/all_to_all | solution.py:135
  304.0 3.8 %copy-start.3 = (f32[4,3,1,49152]{3,0,1,2:T(4,128)S(1)}, f32[4,3,1,49152]{3,0,1,2:T(4,128)}, u32[]{:S(2)}) copy-start(f32[4,3,1,49152]{3,0,1,2:T(4,128)} %get-tuple-element.17) | copy-start | bytes 7077892
  307.9 3.8 %copy-start.2 = (f32[4,3,1,49152]{3,0,1,2:T(4,128)S(1)}, f32[4,3,1,49152]{3,0,1,2:T(4,128)}, u32[]{:S(2)}) copy-start(f32[4,3,1,49152]{3,0,1,2:T(4,128)} %get-tuple-element.18) | copy-start | bytes 7077892
  311.7 7.2 %copy-start.1 = (bf16[256,512]{1,0:T(8,128)(2,1)S(1)}, bf16[256,512]{1,0:T(8,128)(2,1)}, u32[]{:S(2)}) copy-start(bf16[256,512]{1,0:T(8,128)(2,1)} %param.22) | copy-start | bytes 786436
Sparse Core Ops, SparseCore 0:
  157.1 25.6 all-gather.1
where the time goes:
time: 328 us; the launch traced here: 326 us
  waiting for transfers between devices  118 us (36%)
  blocking collectives  104 us (32%)
  matrix products  37.1 us (11%)
  local copies, waits for them, and re-layouts  27.7 us (8%)
  starting transfers between devices  22.8 us (7%)
  between operations  14.9 us (5%)
    psum x1, blocking collectives, shards(): totals = lax.psum(fwd_partial, 'hid')  78.6 us
    all_to_all x1, waiting for transfers between devices, shards(): lax.all_to_all(grads[None].astype(jnp.bfloat16), 'slot', split_axis=2, co...  63.7 us
    all_to_all x1, waiting for transfers between devices, shards(): lax.all_to_all(picked, 'slot', split_axis=0, concat_axis=2, tiled=True)[0]  51.3 us
    psum x1, blocking collectives, shards(): center = lax.psum(jnp.sum(scores), 'slot') / row_total  18.7 us
    unnamed x41, local copies, waits for them, and re-layouts  14.4 us
    dot_general x1, matrix products, shards(): jnp.einsum('es,sabc->eabc', owner_map, arrived, precision=lax.Precision.H...  9.69 us
    all_to_all x1, starting transfers between devices, shards(): lax.all_to_all(buffer_rows, 'slot', split_axis=0, concat_axis=0, tiled=True)  8.61 us
  transfers between devices with their start and end apart: 5, of which 3 were waited for; matrix products, arithmetic and copies ran while one was open for 10% of the time, Pallas kernels for 0%

commit v1 on v0

--- a/solution.py
+++ b/solution.py
@@ -1,6 +1,10 @@
+import functools
+
 import jax
 import jax.numpy as jnp
 from jax import lax
+from jax.experimental import pallas as pl
+from jax.experimental.pallas import tpu as pltpu
 from jax.sharding import PartitionSpec as P
 
 beta_kto = 1.0
@@ -141,9 +145,589 @@
     return (out_rows, new_master, new_first, new_second)
 
 
+ACROSS = (((1,), (1,)), ((), ()))
+F32 = jnp.float32
+BF16 = jnp.bfloat16
+MESH = pl.DeviceIdType.MESH
+ROW_STEP = 256
+
+
+def kto_kernel(
+    slots,
+    hids,
+    owned,
+    experts,
+    place_cur,
+    place_next,
+    rows_in,
+    back_map,
+    ref_ref,
+    sign_ref,
+    w_hbm,
+    x_hbm,
+    r_hbm,
+    mast_hbm,
+    mom1_hbm,
+    mom2_hbm,
+    out_ref,
+    nmast_hbm,
+    nmom1_hbm,
+    nmom2_hbm,
+    w_v,
+    x_v,
+    r_v,
+    mast_v,
+    mom1_v,
+    mom2_v,
+    pre_gate,
+    pre_up,
+    hid_v,
+    d_gu,
+    d_hid,
+    gsend,
+    grecv,
+    wsend,
+    wrecv,
+    rows_full,
+    part_v,
+    part_all,
+    tot_v,
+    tot_all,
+    out_part,
+    lev1,
+    lev2_send,
+    lev2,
+    ret_send,
+    ret_recv,
+    load_sem,
+    xr_sem,
+    mom_sem,
+    store_sem,
+    row_ss,
+    row_rs,
+    gat_ss,
+    gat_rs,
+    part_ss,
+    part_rs,
+    tot_ss,
+    tot_rs,
+    g_ss,
+    g_rs,
+    w_ss,
+    w_rs,
+    l1_ss,
+    l1_rs,
+    l2_ss,
+    l2_rs,
+    ret_ss,
+    ret_rs,
+):
+    me_s = lax.axis_index("slot")
+    me_h = lax.axis_index("hid")
+    width = w_v.shape[2]
+    half = width // 2
+    quarter = rows_in.shape[2]
+    cap = rows_in.shape[1]
+    pair = 2 * owned
+    rows = x_v.shape[0]
+    steps = rows // ROW_STEP
+
+    def slot_peer(k):
+        return lax.rem(me_s + k, slots)
+
+    def hid_peer(k):
+        return lax.rem(me_h + k, hids)
+
+    def remote(src, dst, ssem, rsem, slot=None, hid=None):
+        return pltpu.make_async_remote_copy(
+            src_ref=src,
+            dst_ref=dst,
+            send_sem=ssem,
+            recv_sem=rsem,
+            device_id=(me_s if slot is None else slot, me_h if hid is None else hid),
+            device_id_type=MESH,
+        )
+
+    def loop(low, high, body):
+        def step(i, carry):
+            body(i)
+            return carry
+
+        lax.fori_loop(low, high, step, 0)
+
+    w_load = pltpu.make_async_copy(w_hbm, w_v, load_sem.at[0])
+    w_load.start()
+
+    def xr_copies(c):
+        at = pl.ds(pl.multiple_of(c * ROW_STEP, ROW_STEP), ROW_STEP)
+        return (
+            pltpu.make_async_copy(x_hbm.at[at], x_v.at[at], xr_sem.at[0, c]),
+            pltpu.make_async_copy(r_hbm.at[at], r_v.at[at], xr_sem.at[1, c]),
+        )
+
+    def start_xr(c):
+        for copy in xr_copies(c):
+            copy.start()
+
+    loop(0, steps, start_xr)
+    state = ((mast_hbm, mast_v, nmast_hbm), (mom1_hbm, mom1_v, nmom1_hbm), (mom2_hbm, mom2_v, nmom2_hbm))
+    for i, (src, dst, _) in enumerate(state):
+        pltpu.make_async_copy(src, dst, mom_sem.at[i]).start()
+
+    barrier = pltpu.get_barrier_semaphore()
+
+    def greet_slot(k):
+        pl.semaphore_signal(barrier, inc=1, device_id=(slot_peer(k), me_h), device_id_type=MESH)
+
+    def greet_hid(k):
+        pl.semaphore_signal(barrier, inc=1, device_id=(me_s, hid_peer(k)), device_id_type=MESH)
+
+    loop(1, slots, greet_slot)
+    loop(1, hids, greet_hid)
+    pl.semaphore_wait(barrier, slots + hids - 2)
+
+    def row_copy(to):
+        return remote(
+            rows_in.at[to], rows_full.at[me_h, me_s], row_ss.at[to], row_rs.at[me_s], slot=to
+        )
+
+    loop(1, slots, lambda k: row_copy(slot_peer(k)).start())
+    rows_full[me_h, me_s] = rows_in[me_s]
+
+    w_load.wait()
+
+    def first_half(c):
+        for copy in xr_copies(c):
+            copy.wait()
+        at = pl.ds(pl.multiple_of(c * ROW_STEP, ROW_STEP), ROW_STEP)
+        xc = x_v[at, :]
+        rc = r_v[at, :]
+        gate = lax.dot_general(w_v[0], xc, ACROSS, preferred_element_type=F32)
+        up = lax.dot_general(w_v[1], xc, ACROSS, preferred_element_type=F32)
+        turn = lax.dot_general(w_v[2], rc, ACROSS, preferred_element_type=F32)
+        sig = jax.nn.sigmoid(gate)
+        act = gate * sig
+        hidden = (act * up).astype(BF16).astype(F32)
+        part_v[:, at] = jnp.sum(hidden * turn, axis=0, keepdims=True)
+        pre_gate[:, at] = turn * up * sig * (1.0 + gate * (1.0 - sig))
+        pre_up[:, at] = turn * act
+        hid_v[:, at] = hidden
+
+    loop(0, steps, first_half)
+
+    def part_copy(to):
+        return remote(part_v, part_all.at[me_h], part_ss.at[to], part_rs.at[me_h], hid=to)
+
+    loop(1, hids, lambda k: part_copy(hid_peer(k)).start())
+    part_all[me_h] = part_v[...]
+
+    def part_wait(k):
+        frm = hid_peer(k)
+        remote(part_v, part_all.at[frm], part_ss.at[frm], part_rs.at[frm], hid=frm).wait_recv()
+
+    loop(1, hids, part_wait)
+    policy = part_all[0]
+    for h in range(1, hids):
+        policy = policy + part_all[h]
+    scores = policy - ref_ref[...]
+    tot_v[...] = jnp.broadcast_to(jnp.sum(scores, axis=1, keepdims=True), tot_v.shape)
+
+    def tot_copy(to):
+        return remote(tot_v, tot_all.at[me_s], tot_ss.at[to], tot_rs.at[me_s], slot=to)
+
+    loop(1, slots, lambda k: tot_copy(slot_peer(k)).start())
+    tot_all[me_s] = tot_v[...]
+
+    def tot_wait(k):
+        frm = slot_peer(k)
+        remote(tot_v, tot_all.at[frm], tot_ss.at[frm], tot_rs.at[frm], slot=frm).wait_recv()
+
+    loop(1, slots, tot_wait)
+    total = tot_all[0]
+    for s in range(1, slots):
+        total = total + tot_all[s]
+    center = total[:, :1] * (1.0 / (slots * rows))
+    sigma_v = jax.nn.sigmoid(beta_kto * (scores - center))
+    slope = beta_kto * sigma_v * (1.0 - sigma_v) * sign_ref[...]
+
+    for s in range(slots):
+        units = pl.ds(s * owned, owned)
+        both = jnp.concatenate([pre_gate[units, :] * slope, pre_up[units, :] * slope], axis=0)
+        d_gu[pl.ds(s * pair, pair), :] = both.astype(BF16)
+    d_hid[...] = (hid_v[...] * slope).astype(BF16)
+
+    def grad_copy(p, to):
+        return remote(
+            gsend.at[p, to], grecv.at[p, me_s], g_ss.at[p, to], g_rs.at[p, me_s], slot=to
+        )
+
+    cut = 512
+    per_piece = half // cut
+    for p in range(3):
+
+        def grads(i, p=p):
+            here = pl.ds(pl.multiple_of(i * cut, cut), cut)
+            if p < 2:
+                at = pl.ds(pl.multiple_of(p * half + i * cut, cut), cut)
+                found = jnp.dot(d_gu[...], x_v[:, at], preferred_element_type=F32)
+                gsend[p, :, :, here] = found.astype(BF16).reshape(slots, pair, cut)
+            else:
+                high = pl.ds(pl.multiple_of(half + i * cut, cut), cut)
+                low_part = jnp.dot(d_hid[...], r_v[:, here], preferred_element_type=F32)
+                high_part = jnp.dot(d_hid[...], r_v[:, high], preferred_element_type=F32)
+                both = jnp.concatenate(
+                    [low_part.reshape(slots, owned, cut), high_part.reshape(slots, owned, cut)],
+                    axis=1,
+                )
+                gsend[p, :, :, here] = both.astype(BF16)
+
+        loop(0, per_piece, grads)
+        loop(1, slots, lambda k, p=p: grad_copy(p, slot_peer(k)).start())
+        grecv[p, me_s] = gsend[p, me_s]
+
+    def row_wait(k):
+        frm = slot_peer(k)
+        remote(
+            rows_in.at[frm], rows_full.at[me_h, frm], row_ss.at[frm], row_rs.at[frm], slot=frm
+        ).wait_recv()
+
+    loop(1, slots, row_wait)
+
+    def gather_copy(to):
+        return remote(
+            rows_full.at[me_h], rows_full.at[me_h], gat_ss.at[to], gat_rs.at[me_h], hid=to
+        )
+
+    loop(1, hids, lambda k: gather_copy(hid_peer(k)).start())
+
+    for i, (src, dst, _) in enumerate(state):
+        pltpu.make_async_copy(src, dst, mom_sem.at[i]).wait()
+    cur = [place_cur[s] for s in range(slots)]
+    nxt = [place_next[s] for s in range(slots)]
+    is_cur = [[jnp.where(cur[s] == e, 1.0, 0.0) for s in range(slots)] for e in range(experts)]
+    is_nxt = [[jnp.where(nxt[t] == e, 1.0, 0.0) for t in range(slots)] for e in range(experts)]
+    blocks = width // 128
+    half_blocks = half // 128
+
+    def weight_copy(p, to):
+        return remote(
+            wsend.at[p, to], wrecv.at[p, me_s], w_ss.at[p, to], w_rs.at[p, me_s], slot=to
+        )
+
+    for p in range(3):
+
+        def grad_wait(k, p=p):
+            frm = slot_peer(k)
+            remote(
+                gsend.at[p, frm], grecv.at[p, frm], g_ss.at[p, frm], g_rs.at[p, frm], slot=frm
+            ).wait_recv()
+
+        loop(1, slots, grad_wait)
+
+        def adam(j, p=p):
+            lanes = pl.ds(pl.multiple_of(j * 128, 128), 128)
+            came = [grecv[p, s, :, lanes].astype(F32) for s in range(slots)]
+            fresh = []
+            for e in range(experts):
+                summed = came[0] * is_cur[e][0]
+                for s in range(1, slots):
+                    summed = summed + came[s] * is_cur[e][s]
+                sides = []
+                for side in range(2):
+                    if p < 2:
+                        row, block = e * 3 + side, p * half_blocks + j
+                    else:
+                        row, block = e * 3 + 2, side * half_blocks + j
+                    at = pl.ds(block, owned, stride=blocks)
+                    new_m, new_1, new_2 = adamw_update(
+                        mast_v[row, at, :],
+                        mom1_v[row, at, :],
+                        mom2_v[row, at, :],
+                        summed[side * owned : (side + 1) * owned],
+                    )
+                    mast_v[row, at, :] = new_m
+                    mom1_v[row, at, :] = new_1
+                    mom2_v[row, at, :] = new_2
+                    sides.append(new_m)
+                fresh.append(jnp.concatenate(sides, axis=0))
+            for t in range(slots):
+                chosen = fresh[0] * is_nxt[0][t]
+                for e in range(1, experts):
+                    chosen = chosen + fresh[e] * is_nxt[e][t]
+                wsend[p, t, :, lanes] = chosen.astype(BF16)
+
+        loop(0, half_blocks, adam)
+        loop(1, slots, lambda k, p=p: weight_copy(p, slot_peer(k)).start())
+        wrecv[p, me_s] = wsend[p, me_s]
+    for i, (_, dst, new) in enumerate(state):
+        pltpu.make_async_copy(dst, new, store_sem.at[i]).start()
+
+    def gather_wait(k):
+        frm = hid_peer(k)
+        remote(
+            rows_full.at[frm], rows_full.at[frm], gat_ss.at[frm], gat_rs.at[frm], hid=frm
+        ).wait_recv()
+
+    loop(1, hids, gather_wait)
+
+    def weight_wait(p):
+        def one(k):
+            frm = slot_peer(k)
+            remote(
+                wsend.at[p, frm], wrecv.at[p, frm], w_ss.at[p, frm], w_rs.at[p, frm], slot=frm
+            ).wait_recv()
+
+        loop(1, slots, one)
+
+    taken = slots * cap
+    mixed = None
+    for h in range(hids):
+        p, inner = divmod(h * quarter, half)
+        if inner == 0:
+            weight_wait(p)
+        mat = wrecv[p, :, :, inner : inner + quarter].reshape(slots * pair, quarter)
+        term = lax.dot_general(
+            mat, rows_full[h].reshape(taken, quarter), ACROSS, preferred_element_type=F32
+        )
+        mixed = term if mixed is None else mixed + term
+    mixed = mixed.reshape(slots, pair, taken)
+    gate = mixed[:, :owned]
+    hidden = gate * jax.nn.sigmoid(gate) * mixed[:, owned:]
+    blank = jnp.zeros_like(hidden)
+    low_hid = jnp.concatenate([hidden, blank], axis=1).reshape(slots * pair, taken)
+    high_hid = jnp.concatenate([blank, hidden], axis=1).reshape(slots * pair, taken)
+    low_hid = jnp.transpose(low_hid).astype(BF16)
+    high_hid = jnp.transpose(high_hid).astype(BF16)
+    weight_wait(2)
+    for b in range(hids):
+        side, inner = divmod(b * quarter, half)
+        mat = wrecv[2, :, :, inner : inner + quarter].reshape(slots * pair, quarter)
+        got = jnp.dot(low_hid if side == 0 else high_hid, mat, preferred_element_type=F32)
+        out_part[b] = got.astype(BF16).reshape(slots, cap, quarter)
+
+    pos = lax.rem(me_h, 2)
+    grp = me_h // 2
+    mate = grp * 2 + 1 - pos
+    far = (1 - grp) * 2 + pos
+
+    def lev1_copy(g):
+        return remote(
+            out_part.at[2 * g + 1 - pos], lev1.at[g], l1_ss.at[g], l1_rs.at[g], hid=mate
+        )
+
+    lev1_copy(1 - grp).start()
+    lev1_copy(grp).start()
+    lev1_copy(1 - grp).wait_recv()
+
+    def lev2_copy(s):
+        return remote(lev2_send.at[s], lev2.at[s], l2_ss.at[s], l2_rs.at[s], hid=far)
+
+    def to_far(k):
+        s = slot_peer(k)
+        both = out_part[far, s].astype(F32) + lev1[1 - grp, s].astype(F32)
+        lev2_send[s] = both.astype(BF16)
+        lev2_copy(s).start()
+
+    loop(1, slots + 1, to_far)
+    lev1_copy(grp).wait_recv()
+
+    def ret_copy(to):
+        return remote(
+            ret_send.at[to], ret_recv.at[me_s], ret_ss.at[to], ret_rs.at[me_s], slot=to
+        )
+
+    def last_sum(s):
+        lev2_copy(s).wait_recv()
+        own = out_part[me_h, s].astype(F32) + lev1[grp, s].astype(F32)
+        return (own + lev2[s].astype(F32)).astype(BF16)
+
+    def give_back(k):
+        s = slot_peer(k)
+        ret_send[s] = last_sum(s)
+        ret_copy(s).start()
+
+    loop(1, slots, give_back)
+    ret_recv[me_s] = last_sum(me_s)
+
+    def ret_wait(k):
+        frm = slot_peer(k)
+        remote(
+            ret_send.at[frm], ret_recv.at[frm], ret_ss.at[frm], ret_rs.at[frm], slot=frm
+        ).wait_recv()
+
+    loop(1, slots, ret_wait)
+    out_ref[...] = jnp.dot(
+        back_map[...], ret_recv[...].reshape(taken, quarter), preferred_element_type=F32
+    ).astype(BF16)
+
+    def slot_sends(k):
+        to = slot_peer(k)
+        row_copy(to).wait_send()
+        tot_copy(to).wait_send()
+        for p in range(3):
+            grad_copy(p, to).wait_send()
+            weight_copy(p, to).wait_send()
+        ret_copy(to).wait_send()
+
+    def hid_sends(k):
+        to = hid_peer(k)
+        part_copy(to).wait_send()
+        gather_copy(to).wait_send()
+
+    loop(1, slots, slot_sends)
+    loop(1, hids, hid_sends)
+    loop(0, slots, lambda s: lev2_copy(s).wait_send())
+    for g in range(2):
+        lev1_copy(g).wait_send()
+    for i, (_, dst, new) in enumerate(state):
+        pltpu.make_async_copy(dst, new, store_sem.at[i]).wait()
+
+
+def fused_shards(
+    master,
+    first_moment,
+    second_moment,
+    slot_weights,
+    back_rows,
+    readout,
+    ref_logratio,
+    labels,
+    place_cur,
+    place_next,
+    fwd_rows,
+    routes,
+):
+    slots = lax.axis_size("slot")
+    hids = lax.axis_size("hid")
+    experts = master.shape[0]
+    _, kinds, units, width = slot_weights.shape
+    owned = units // slots
+    rows = back_rows.shape[1]
+    half = width // 2
+    quarter = fwd_rows.shape[1]
+    cap = 2 * fwd_rows.shape[0] // slots
+    taken = slots * cap
+    target = routes[:, 0]
+    target_map = (target[:, None] == jnp.arange(slots, dtype=jnp.int32)[None, :]).astype(jnp.int32)
+    earlier = jnp.cumsum(target_map, axis=0) - target_map
+    position = jnp.sum(earlier * target_map, axis=1)
+    slot_place = target * cap + position
+    back_map = (slot_place[:, None] == jnp.arange(taken, dtype=jnp.int32)[None, :]).astype(BF16)
+    buffer_rows = lax.dot_general(
+        back_map, fwd_rows, (((0,), (0,)), ((), ())), preferred_element_type=F32
+    ).astype(BF16)
+    sign = jnp.where(labels == 1, -desired_weight, undesired_weight).astype(F32)
+    lines = (experts * kinds, owned * width // 128, 128)
+    vmem = pl.BlockSpec(memory_space=pltpu.VMEM)
+    smem = pl.BlockSpec(memory_space=pltpu.SMEM)
+    anywhere = pl.BlockSpec(memory_space=pl.ANY)
+    pieces = (3, slots, 2 * owned, half)
+    dma = pltpu.SemaphoreType.DMA
+    scratch = [
+        pltpu.VMEM((kinds, units, width), BF16),
+        pltpu.VMEM((rows, width), BF16),
+        pltpu.VMEM((rows, width), BF16),
+        pltpu.VMEM(lines, F32),
+        pltpu.VMEM(lines, F32),
+        pltpu.VMEM(lines, F32),
+        pltpu.VMEM((units, rows), F32),
+        pltpu.VMEM((units, rows), F32),
+        pltpu.VMEM((units, rows), F32),
+        pltpu.VMEM((2 * units, rows), BF16),
+        pltpu.VMEM((units, rows), BF16),
+        pltpu.VMEM(pieces, BF16),
+        pltpu.VMEM(pieces, BF16),
+        pltpu.VMEM(pieces, BF16),
+        pltpu.VMEM(pieces, BF16),
+        pltpu.VMEM((hids, slots, cap, quarter), BF16),
+        pltpu.VMEM((1, rows), F32),
+        pltpu.VMEM((hids, 1, rows), F32),
+        pltpu.VMEM((1, 128), F32),
+        pltpu.VMEM((slots, 1, 128), F32),
+        pltpu.VMEM((hids, slots, cap, quarter), BF16),
+        pltpu.VMEM((2, slots, cap, quarter), BF16),
+        pltpu.VMEM((slots, cap, quarter), BF16),
+        pltpu.VMEM((slots, cap, quarter), BF16),
+        pltpu.VMEM((slots, cap, quarter), BF16),
+        pltpu.VMEM((slots, cap, quarter), BF16),
+        dma((1,)),
+        dma((2, rows // ROW_STEP)),
+        dma((3,)),
+        dma((3,)),
+        dma((slots,)),
+        dma((slots,)),
+        dma((hids,)),
+        dma((hids,)),
+        dma((hids,)),
+        dma((hids,)),
+        dma((slots,)),
+        dma((slots,)),
+        dma((3, slots)),
+        dma((3, slots)),
+        dma((3, slots)),
+        dma((3, slots)),
+        dma((2,)),
+        dma((2,)),
+        dma((slots,)),
+        dma((slots,)),
+        dma((slots,)),
+        dma((slots,)),
+    ]
+    state_shape = jax.ShapeDtypeStruct(lines, F32)
+    out_rows, new_master, new_first, new_second = pl.pallas_call(
+        functools.partial(kto_kernel, slots, hids, owned, experts),
+        out_shape=(
+            jax.ShapeDtypeStruct(fwd_rows.shape, BF16),
+            state_shape,
+            state_shape,
+            state_shape,
+        ),
+        in_specs=[smem, smem, vmem, vmem, vmem, vmem] + [anywhere] * 6,
+        out_specs=(vmem, anywhere, anywhere, anywhere),
+        scratch_shapes=scratch,
+        compiler_params=pltpu.CompilerParams(
+            collective_id=0, has_side_effects=True, vmem_limit_bytes=VMEM_BYTES
+        ),
+        cost_estimate=pl.CostEstimate(
+            flops=2 * (6 * rows + 3 * taken) * units * width,
+            bytes_accessed=24 * master.size + 4 * rows * width,
+            transcendentals=2 * rows * units,
+        ),
+    )(
+        place_cur,
+        place_next,
+        buffer_rows.reshape(slots, cap, quarter),
+        back_map,
+        ref_logratio,
+        sign,
+        slot_weights[0],
+        back_rows[0],
+        readout[0],
+        master.reshape(lines),
+        first_moment.reshape(lines),
+        second_moment.reshape(lines),
+    )
+    shape = master.shape
+    return (out_rows, new_master.reshape(shape), new_first.reshape(shape), new_second.reshape(shape))
+
+
+VMEM_BYTES = 60 * 1024 * 1024
+
+
+def step(*arrays):
+    slots = lax.axis_size("slot")
+    weights, fwd_rows = arrays[3], arrays[10]
+    owned = weights.shape[2] // slots
+    cap = 2 * fwd_rows.shape[0] // slots
+    fits = owned % 8 == 0 and cap % 16 == 0 and lax.axis_size("hid") == 4
+    fits = fits and weights.shape[3] == 4 * fwd_rows.shape[1] and weights.shape[3] % 1024 == 0
+    fits = fits and arrays[4].shape[1] % ROW_STEP == 0
+    return (fused_shards if fits else shards)(*arrays)
+
+
 def solution(mesh):
     return jax.shard_map(
-        shards,
+        step,
         mesh=mesh,
         in_specs=(
             P(None, None, "hid", "slot"),

time: 328 us -> 160 us (0.49)
  Pallas kernels: 0 us -> 142 us
  waiting for transfers between devices: 118 us -> 0 us
  blocking collectives: 104 us -> 0 us
  matrix products: 37.1 us -> 1.22 us
  starting transfers between devices: 22.8 us -> 0 us
  local copies, waits for them, and re-layouts: 27.7 us -> 9.19 us
  between operations: 14.9 us -> 0.66 us
  other arithmetic: 1.6 us -> 4.89 us
    pallas_call x0 -> x1, Pallas kernels: none -> 142 us  [fused_shards(): pl.pallas_call(functools.partial(kto_kernel, slots, hids, owned, experts)...]
    all_to_all x4 -> x0, waiting for transfers between devices: 117 us -> none  [the longest x1 63.7 us: shards(): lax.all_to_all(grads[None].astype(jnp.bfloat16), 'slot', split_axis=2, co...]
    psum x3 -> x0, blocking collectives: 104 us -> none  [the longest x1 78.6 us: shards(): totals = lax.psum(fwd_partial, 'hid')]
    dot_general x13 -> x1, matrix products: 37.1 us -> 1.22 us  [fused_shards(): lax.dot_general(back_map, fwd_rows, (((0,), (0,)), ((), ())), preferred_e...]
    all_to_all x4 -> x0, starting transfers between devices: 22.7 us -> none  [the longest x1 8.61 us: shards(): lax.all_to_all(buffer_rows, 'slot', split_axis=0, concat_axis=0, tiled=True)]
    unnamed x41 -> x10, local copies, waits for them, and re-layouts: 14.4 us -> 8.98 us
    another operation x2 -> x1, local copies, waits for them, and re-layouts: 3.68 us -> 0.01 us  [the longest x1 3.67 us: expert_backward(): return jnp.stack([grad_gate, grad_up, grad_down])]
    all_to_all x2 -> x0, local copies, waits for them, and re-layouts: 3.53 us -> none  [the longest x1 1.82 us: shards(): lax.all_to_all(picked, 'slot', split_axis=0, concat_axis=2, tiled=True)[0]]
  transfers between devices with their start and end apart: 5 -> 0, of which waited for: 3 -> 0; matrix products, arithmetic and copies ran while one was open for 10% -> 0% of each run, Pallas kernels for 0% -> 0%
where the time goes in v1:
time: 160 us; the launch traced here: 158 us
  Pallas kernels  142 us (89%)
  local copies, waits for them, and re-layouts  9.19 us (6%)
  other arithmetic  4.89 us (3%)
    pallas_call x1, Pallas kernels, fused_shards(): pl.pallas_call(functools.partial(kto_kernel, slots, hids, owned, experts)...  142 us
    unnamed x10, local copies, waits for them, and re-layouts  8.98 us

profile of v1, /device:TPU:1, one launch (start us, length us, event | category | flops | bytes accessed | tf_op | source)
XLA Modules:
  0.0 157.9 jit_solution(11302962557061612839)
XLA Ops:
  0.6 0.0 copy-start
  0.6 1.3 compare_select_fusion.sign_ref
  2.0 0.7 fusion.4
  2.7 0.6 reduce-window.6
  3.2 0.2 slice_reduce_fusion
  3.5 0.8 fusion.3
  4.3 0.7 multiply_add_fusion
  4.9 0.8 fusion.back_map
  5.8 0.0 copy-done
  5.8 1.2 convolution_convert_fusion
  7.0 142.0 %shard_map.147 = (bf16[256,512]{1,0:T(8,128)(2,1)}, f32[12,384,128]{2,1,0:T(8,128)}, f32[12,384,128]{2,1,0:T(8,128)}, f32[12,384,128]{2,1,0:T(8,128)}) custom-call(s32[8]{0:T(128)} %place_cur.1, s32[8]{0:T(128)} %place_next.1, bf16[8,64,512]{2,1,0:T(8,128)(2,1)} %bitcast.26, bf16[256,512]{1,0:T(8,128)(2,1)} %fusion.back_map, f32[1,1024]{1,0:T(1,128)} %ref_ref.1, ...), custom_call_target="tpu_custom_call" | custom-call | flops 6039797760 | bytes 22544384 | tf_op jit(solution)/shard_map/pallas_call | solution.py:677
  148.9 1.7 %copy.26 = bf16[256,512]{1,0:T(8,128)(2,1)} copy(bf16[256,512]{1,0:T(8,128)(2,1)} %get-tuple-element.24) | data formatting | bytes 524288
  150.6 0.0 copy-start.2
  150.6 3.4 %copy.27 = f32[4,3,1,49152]{3,2,1,0:T(1,128)} copy(f32[4,3,1,49152]{3,2,1,0:T(1,128)} %bitcast.25) | data formatting | bytes 4718592
  154.0 0.0 copy-done.2
  154.0 0.0 copy-start.1
  154.0 1.4 copy.28
  155.4 1.1 copy-done.1
  156.5 1.4 copy.29
  (2 shorter events, 0.0 us)
Async XLA Ops:
  0.6 5.1 %copy-start = (bf16[256,512]{1,0:T(8,128)(2,1)S(1)}, bf16[256,512]{1,0:T(8,128)(2,1)}, u32[]{:S(2)}) copy-start(bf16[256,512]{1,0:T(8,128)(2,1)} %param.22) | copy-start | bytes 786436
  150.6 3.4 %copy-start.2 = (f32[12,384,128]{2,1,0:T(8,128)S(1)}, f32[12,384,128]{2,1,0:T(8,128)}, u32[]{:S(2)}) copy-start(f32[12,384,128]{2,1,0:T(8,128)} %get-tuple-element.10) | copy-start | bytes 7077892
  154.0 2.5 %copy-start.1 = (f32[12,384,128]{2,1,0:T(8,128)S(1)}, f32[12,384,128]{2,1,0:T(8,128)}, u32[]{:S(2)}) copy-start(f32[12,384,128]{2,1,0:T(8,128)} %get-tuple-element.11) | copy-start | bytes 7077892

commit v2 on v1

--- a/solution.py
+++ b/solution.py
@@ -159,10 +159,10 @@
     experts,
     place_cur,
     place_next,
-    rows_in,
-    back_map,
+    route_ref,
+    label_ref,
     ref_ref,
-    sign_ref,
+    fwd_hbm,
     w_hbm,
     x_hbm,
     r_hbm,
@@ -173,6 +173,9 @@
     nmast_hbm,
     nmom1_hbm,
     nmom2_hbm,
+    fwd_v,
+    rows_in,
+    back_map,
     w_v,
     x_v,
     r_v,
@@ -193,6 +196,7 @@
     part_all,
     tot_v,
     tot_all,
+    side_hid,
     out_part,
     lev1,
     lev2_send,
@@ -228,8 +232,11 @@
     half = width // 2
     quarter = rows_in.shape[2]
     cap = rows_in.shape[1]
+    taken = slots * cap
     pair = 2 * owned
     rows = x_v.shape[0]
+    mixing = width // quarter
+    pieces = mixing + half // quarter
     steps = rows // ROW_STEP
 
     def slot_peer(k):
@@ -255,6 +262,8 @@
 
         lax.fori_loop(low, high, step, 0)
 
+    fwd_load = pltpu.make_async_copy(fwd_hbm, fwd_v, load_sem.at[1])
+    fwd_load.start()
     w_load = pltpu.make_async_copy(w_hbm, w_v, load_sem.at[0])
     w_load.start()
 
@@ -284,6 +293,23 @@
 
     loop(1, slots, greet_slot)
     loop(1, hids, greet_hid)
+
+    count = fwd_v.shape[0]
+    named = jnp.broadcast_to(route_ref[...].astype(F32), (count, count))
+    first = lax.broadcasted_iota(jnp.int32, (count, count), 0)
+    second = lax.broadcasted_iota(jnp.int32, (count, count), 1)
+    before = (named == jnp.transpose(named)) & (first < second)
+    rank = jnp.sum(jnp.where(before, 1.0, 0.0), axis=0, keepdims=True)
+    place = named[:1] * cap + rank
+    spot = lax.broadcasted_iota(jnp.int32, (taken, count), 0).astype(F32)
+    place_map = jnp.where(spot == place, 1.0, 0.0)
+    back_map[...] = jnp.transpose(place_map).astype(BF16)
+    fwd_load.wait()
+    rows_in[...] = (
+        jnp.dot(place_map.astype(BF16), fwd_v[...], preferred_element_type=F32)
+        .astype(BF16)
+        .reshape(slots, cap, quarter)
+    )
     pl.semaphore_wait(barrier, slots + hids - 2)
 
     def row_copy(to):
@@ -347,8 +373,7 @@
     for s in range(1, slots):
         total = total + tot_all[s]
     center = total[:, :1] * (1.0 / (slots * rows))
-    sigma_v = jax.nn.sigmoid(beta_kto * (scores - center))
-    slope = beta_kto * sigma_v * (1.0 - sigma_v) * sign_ref[...]
+    slope = kto_slope(scores, label_ref[...], center)
 
     for s in range(slots):
         units = pl.ds(s * owned, owned)
@@ -361,29 +386,30 @@
             gsend.at[p, to], grecv.at[p, me_s], g_ss.at[p, to], g_rs.at[p, me_s], slot=to
         )
 
-    cut = 512
-    per_piece = half // cut
-    for p in range(3):
-
-        def grads(i, p=p):
-            here = pl.ds(pl.multiple_of(i * cut, cut), cut)
-            if p < 2:
-                at = pl.ds(pl.multiple_of(p * half + i * cut, cut), cut)
-                found = jnp.dot(d_gu[...], x_v[:, at], preferred_element_type=F32)
-                gsend[p, :, :, here] = found.astype(BF16).reshape(slots, pair, cut)
-            else:
-                high = pl.ds(pl.multiple_of(half + i * cut, cut), cut)
-                low_part = jnp.dot(d_hid[...], r_v[:, here], preferred_element_type=F32)
-                high_part = jnp.dot(d_hid[...], r_v[:, high], preferred_element_type=F32)
-                both = jnp.concatenate(
-                    [low_part.reshape(slots, owned, cut), high_part.reshape(slots, owned, cut)],
-                    axis=1,
-                )
-                gsend[p, :, :, here] = both.astype(BF16)
-
-        loop(0, per_piece, grads)
-        loop(1, slots, lambda k, p=p: grad_copy(p, slot_peer(k)).start())
+    def send_grads(p):
+        loop(1, slots, lambda k: grad_copy(p, slot_peer(k)).start())
         grecv[p, me_s] = gsend[p, me_s]
+
+    def mixing_grads(p):
+        at = pl.ds(pl.multiple_of(p * quarter, quarter), quarter)
+        found = jnp.dot(d_gu[...], x_v[:, at], preferred_element_type=F32)
+        gsend[p] = found.astype(BF16).reshape(slots, pair, quarter)
+        send_grads(p)
+
+    def down_grads(p):
+        low = pl.ds(pl.multiple_of((p - mixing) * quarter, quarter), quarter)
+        high = pl.ds(pl.multiple_of(half + (p - mixing) * quarter, quarter), quarter)
+        low_part = jnp.dot(d_hid[...], r_v[:, low], preferred_element_type=F32)
+        high_part = jnp.dot(d_hid[...], r_v[:, high], preferred_element_type=F32)
+        both = jnp.concatenate(
+            [low_part.reshape(slots, owned, quarter), high_part.reshape(slots, owned, quarter)],
+            axis=1,
+        )
+        gsend[p] = both.astype(BF16)
+        send_grads(p)
+
+    loop(0, mixing, mixing_grads)
+    loop(mixing, pieces, down_grads)
 
     def row_wait(k):
         frm = slot_peer(k)
@@ -407,16 +433,15 @@
     is_cur = [[jnp.where(cur[s] == e, 1.0, 0.0) for s in range(slots)] for e in range(experts)]
     is_nxt = [[jnp.where(nxt[t] == e, 1.0, 0.0) for t in range(slots)] for e in range(experts)]
     blocks = width // 128
-    half_blocks = half // 128
+    part_blocks = quarter // 128
 
     def weight_copy(p, to):
         return remote(
             wsend.at[p, to], wrecv.at[p, me_s], w_ss.at[p, to], w_rs.at[p, me_s], slot=to
         )
 
-    for p in range(3):
-
-        def grad_wait(k, p=p):
+    def adam(p, spots):
+        def grad_wait(k):
             frm = slot_peer(k)
             remote(
                 gsend.at[p, frm], grecv.at[p, frm], g_ss.at[p, frm], g_rs.at[p, frm], slot=frm
@@ -424,7 +449,7 @@
 
         loop(1, slots, grad_wait)
 
-        def adam(j, p=p):
+        def lane_block(j):
             lanes = pl.ds(pl.multiple_of(j * 128, 128), 128)
             came = [grecv[p, s, :, lanes].astype(F32) for s in range(slots)]
             fresh = []
@@ -433,11 +458,8 @@
                 for s in range(1, slots):
                     summed = summed + came[s] * is_cur[e][s]
                 sides = []
-                for side in range(2):
-                    if p < 2:
-                        row, block = e * 3 + side, p * half_blocks + j
-                    else:
-                        row, block = e * 3 + 2, side * half_blocks + j
+                for side, (kind, block) in enumerate(spots(j)):
+                    row = e * 3 + kind
                     at = pl.ds(block, owned, stride=blocks)
                     new_m, new_1, new_2 = adamw_update(
                         mast_v[row, at, :],
@@ -456,9 +478,19 @@
                     chosen = chosen + fresh[e] * is_nxt[e][t]
                 wsend[p, t, :, lanes] = chosen.astype(BF16)
 
-        loop(0, half_blocks, adam)
-        loop(1, slots, lambda k, p=p: weight_copy(p, slot_peer(k)).start())
+        loop(0, part_blocks, lane_block)
+        loop(1, slots, lambda k: weight_copy(p, slot_peer(k)).start())
         wrecv[p, me_s] = wsend[p, me_s]
+
+    def mixing_adam(p):
+        adam(p, lambda j: [(side, p * part_blocks + j) for side in range(2)])
+
+    def down_adam(p):
+        start = (p - mixing) * part_blocks
+        adam(p, lambda j: [(2, side * (blocks // 2) + start + j) for side in range(2)])
+
+    loop(0, mixing, mixing_adam)
+    loop(mixing, pieces, down_adam)
     for i, (_, dst, new) in enumerate(state):
         pltpu.make_async_copy(dst, new, store_sem.at[i]).start()
 
@@ -479,15 +511,14 @@
 
         loop(1, slots, one)
 
-    taken = slots * cap
     mixed = None
     for h in range(hids):
-        p, inner = divmod(h * quarter, half)
-        if inner == 0:
-            weight_wait(p)
-        mat = wrecv[p, :, :, inner : inner + quarter].reshape(slots * pair, quarter)
+        weight_wait(h)
         term = lax.dot_general(
-            mat, rows_full[h].reshape(taken, quarter), ACROSS, preferred_element_type=F32
+            wrecv[h].reshape(slots * pair, quarter),
+            rows_full[h].reshape(taken, quarter),
+            ACROSS,
+            preferred_element_type=F32,
         )
         mixed = term if mixed is None else mixed + term
     mixed = mixed.reshape(slots, pair, taken)
@@ -496,31 +527,24 @@
     blank = jnp.zeros_like(hidden)
     low_hid = jnp.concatenate([hidden, blank], axis=1).reshape(slots * pair, taken)
     high_hid = jnp.concatenate([blank, hidden], axis=1).reshape(slots * pair, taken)
-    low_hid = jnp.transpose(low_hid).astype(BF16)
-    high_hid = jnp.transpose(high_hid).astype(BF16)
-    weight_wait(2)
-    for b in range(hids):
-        side, inner = divmod(b * quarter, half)
-        mat = wrecv[2, :, :, inner : inner + quarter].reshape(slots * pair, quarter)
-        got = jnp.dot(low_hid if side == 0 else high_hid, mat, preferred_element_type=F32)
-        out_part[b] = got.astype(BF16).reshape(slots, cap, quarter)
+    side_hid[0] = jnp.transpose(low_hid).astype(BF16)
+    side_hid[1] = jnp.transpose(high_hid).astype(BF16)
 
     pos = lax.rem(me_h, 2)
     grp = me_h // 2
     mate = grp * 2 + 1 - pos
     far = (1 - grp) * 2 + pos
 
-    def lev1_copy(g):
-        return remote(
-            out_part.at[2 * g + 1 - pos], lev1.at[g], l1_ss.at[g], l1_rs.at[g], hid=mate
-        )
-
-    lev1_copy(1 - grp).start()
-    lev1_copy(grp).start()
-    lev1_copy(1 - grp).wait_recv()
+    def lev1_copy(g, turn):
+        return remote(out_part.at[2 * g + turn], lev1.at[g], l1_ss.at[g], l1_rs.at[g], hid=mate)
 
     def lev2_copy(s):
         return remote(lev2_send.at[s], lev2.at[s], l2_ss.at[s], l2_rs.at[s], hid=far)
+
+    def ret_copy(to):
+        return remote(
+            ret_send.at[to], ret_recv.at[me_s], ret_ss.at[to], ret_rs.at[me_s], slot=to
+        )
 
     def to_far(k):
         s = slot_peer(k)
@@ -528,14 +552,6 @@
         lev2_send[s] = both.astype(BF16)
         lev2_copy(s).start()
 
-    loop(1, slots + 1, to_far)
-    lev1_copy(grp).wait_recv()
-
-    def ret_copy(to):
-        return remote(
-            ret_send.at[to], ret_recv.at[me_s], ret_ss.at[to], ret_rs.at[me_s], slot=to
-        )
-
     def last_sum(s):
         lev2_copy(s).wait_recv()
         own = out_part[me_h, s].astype(F32) + lev1[grp, s].astype(F32)
@@ -546,8 +562,28 @@
         ret_send[s] = last_sum(s)
         ret_copy(s).start()
 
-    loop(1, slots, give_back)
-    ret_recv[me_s] = last_sum(me_s)
+    for turn in range(2):
+        weight_wait(mixing + turn)
+        for i in range(2):
+            g = 1 - grp if i == 0 else grp
+            got = jnp.dot(
+                side_hid[g],
+                wrecv[mixing + turn].reshape(slots * pair, quarter),
+                preferred_element_type=F32,
+            )
+            out_part[2 * g + turn] = got.astype(BF16).reshape(slots, cap, quarter)
+
+            @pl.when(pos != turn)
+            def _(g=g, turn=turn):
+                lev1_copy(g, turn).start()
+
+        @pl.when(pos == turn)
+        def _(turn=turn):
+            lev1_copy(1 - grp, turn).wait_recv()
+            loop(1, slots + 1, to_far)
+            lev1_copy(grp, turn).wait_recv()
+            loop(1, slots, give_back)
+            ret_recv[me_s] = last_sum(me_s)
 
     def ret_wait(k):
         frm = slot_peer(k)
@@ -564,7 +600,7 @@
         to = slot_peer(k)
         row_copy(to).wait_send()
         tot_copy(to).wait_send()
-        for p in range(3):
+        for p in range(pieces):
             grad_copy(p, to).wait_send()
             weight_copy(p, to).wait_send()
         ret_copy(to).wait_send()
@@ -578,9 +614,35 @@
     loop(1, hids, hid_sends)
     loop(0, slots, lambda s: lev2_copy(s).wait_send())
     for g in range(2):
-        lev1_copy(g).wait_send()
+        lev1_copy(g, 1 - pos).wait_send()
     for i, (_, dst, new) in enumerate(state):
         pltpu.make_async_copy(dst, new, store_sem.at[i]).wait()
+
+
+def results_kernel(rows_ref, mast_in, mom1_in, mom2_in, out_ref, mast_out, mom1_out, mom2_out, held, sem):
+    parts = sem.shape[2]
+    size = held.shape[1] // parts
+
+    src = (mast_in, mom1_in, mom2_in)
+    dst = (mast_out, mom1_out, mom2_out)
+
+    def come(i, c):
+        at = pl.ds(c * size, size)
+        return pltpu.make_async_copy(src[i].at[at], held.at[i, at], sem.at[0, i, c])
+
+    def go(i, c):
+        at = pl.ds(c * size, size)
+        return pltpu.make_async_copy(held.at[i, at], dst[i].at[at], sem.at[1, i, c])
+
+    every = [(i, c) for i in range(3) for c in range(parts)]
+    for i, c in every:
+        come(i, c).start()
+    out_ref[...] = rows_ref[...]
+    for i, c in every:
+        come(i, c).wait()
+        go(i, c).start()
+    for i, c in every:
+        go(i, c).wait()
 
 
 def fused_shards(
@@ -607,23 +669,16 @@
     quarter = fwd_rows.shape[1]
     cap = 2 * fwd_rows.shape[0] // slots
     taken = slots * cap
-    target = routes[:, 0]
-    target_map = (target[:, None] == jnp.arange(slots, dtype=jnp.int32)[None, :]).astype(jnp.int32)
-    earlier = jnp.cumsum(target_map, axis=0) - target_map
-    position = jnp.sum(earlier * target_map, axis=1)
-    slot_place = target * cap + position
-    back_map = (slot_place[:, None] == jnp.arange(taken, dtype=jnp.int32)[None, :]).astype(BF16)
-    buffer_rows = lax.dot_general(
-        back_map, fwd_rows, (((0,), (0,)), ((), ())), preferred_element_type=F32
-    ).astype(BF16)
-    sign = jnp.where(labels == 1, -desired_weight, undesired_weight).astype(F32)
     lines = (experts * kinds, owned * width // 128, 128)
     vmem = pl.BlockSpec(memory_space=pltpu.VMEM)
     smem = pl.BlockSpec(memory_space=pltpu.SMEM)
     anywhere = pl.BlockSpec(memory_space=pl.ANY)
-    pieces = (3, slots, 2 * owned, half)
+    pieces = (width // quarter + half // quarter, slots, 2 * owned, quarter)
     dma = pltpu.SemaphoreType.DMA
     scratch = [
+        pltpu.VMEM(fwd_rows.shape, BF16),
+        pltpu.VMEM((slots, cap, quarter), BF16),
+        pltpu.VMEM((fwd_rows.shape[0], taken), BF16),
         pltpu.VMEM((kinds, units, width), BF16),
         pltpu.VMEM((rows, width), BF16),
         pltpu.VMEM((rows, width), BF16),
@@ -644,13 +699,14 @@
         pltpu.VMEM((hids, 1, rows), F32),
         pltpu.VMEM((1, 128), F32),
         pltpu.VMEM((slots, 1, 128), F32),
+        pltpu.VMEM((2, taken, 2 * units), BF16),
         pltpu.VMEM((hids, slots, cap, quarter), BF16),
         pltpu.VMEM((2, slots, cap, quarter), BF16),
         pltpu.VMEM((slots, cap, quarter), BF16),
         pltpu.VMEM((slots, cap, quarter), BF16),
         pltpu.VMEM((slots, cap, quarter), BF16),
         pltpu.VMEM((slots, cap, quarter), BF16),
-        dma((1,)),
+        dma((2,)),
         dma((2, rows // ROW_STEP)),
         dma((3,)),
         dma((3,)),
@@ -662,10 +718,10 @@
         dma((hids,)),
         dma((slots,)),
         dma((slots,)),
-        dma((3, slots)),
-        dma((3, slots)),
-        dma((3, slots)),
-        dma((3, slots)),
+        dma(pieces[:2]),
+        dma(pieces[:2]),
+        dma(pieces[:2]),
+        dma(pieces[:2]),
         dma((2,)),
         dma((2,)),
         dma((slots,)),
@@ -682,7 +738,7 @@
             state_shape,
             state_shape,
         ),
-        in_specs=[smem, smem, vmem, vmem, vmem, vmem] + [anywhere] * 6,
+        in_specs=[smem, smem, vmem, vmem, vmem] + [anywhere] * 7,
         out_specs=(vmem, anywhere, anywhere, anywhere),
         scratch_shapes=scratch,
         compiler_params=pltpu.CompilerParams(
@@ -696,10 +752,10 @@
     )(
         place_cur,
         place_next,
-        buffer_rows.reshape(slots, cap, quarter),
-        back_map,
+        routes.reshape(1, fwd_rows.shape[0]),
+        labels,
         ref_logratio,
-        sign,
+        fwd_rows,
         slot_weights[0],
         back_rows[0],
         readout[0],
@@ -707,6 +763,22 @@
         first_moment.reshape(lines),
         second_moment.reshape(lines),
     )
+    out_rows, new_master, new_first, new_second = pl.pallas_call(
+        results_kernel,
+        out_shape=(
+            jax.ShapeDtypeStruct(fwd_rows.shape, BF16),
+            state_shape,
+            state_shape,
+            state_shape,
+        ),
+        in_specs=[vmem] + [anywhere] * 3,
+        out_specs=(vmem, anywhere, anywhere, anywhere),
+        scratch_shapes=[pltpu.VMEM((3,) + lines, F32), dma((2, 3, experts))],
+        compiler_params=pltpu.CompilerParams(vmem_limit_bytes=VMEM_BYTES),
+        cost_estimate=pl.CostEstimate(
+            flops=0, bytes_accessed=24 * master.size, transcendentals=0
+        ),
+    )(out_rows, new_master, new_first, new_second)
     shape = master.shape
     return (out_rows, new_master.reshape(shape), new_first.reshape(shape), new_second.reshape(shape))
 

time: 160 us -> 152 us (0.950)
  local copies, waits for them, and re-layouts: 9.19 us -> 0 us
  Pallas kernels: 142 us -> 151 us
  other arithmetic: 4.89 us -> 0 us
    unnamed x10 -> x0, local copies, waits for them, and re-layouts: 8.98 us -> none
    pallas_call x0 -> x1, Pallas kernels: none -> 7.43 us  [fused_shards(): pl.pallas_call(results_kernel, out_shape=(jax.ShapeDtypeStruct(fwd_rows.s...]
where the time goes in v2:
time: 152 us; the launch traced here: 151 us
  Pallas kernels  151 us (99%)
    pallas_call x1, Pallas kernels, fused_shards(): pl.pallas_call(functools.partial(kto_kernel, slots, hids, owned, experts)...  143 us
    pallas_call x1, Pallas kernels, fused_shards(): pl.pallas_call(results_kernel, out_shape=(jax.ShapeDtypeStruct(fwd_rows.s...  7.43 us

profile of v2, /device:TPU:1, one launch (start us, length us, event | category | flops | bytes accessed | tf_op | source)
XLA Modules:
  0.0 151.4 jit_solution(7143311523316729008)
XLA Ops:
  0.6 143.3 %shard_map.147 = (bf16[256,512]{1,0:T(8,128)(2,1)}, f32[12,384,128]{2,1,0:T(8,128)}, f32[12,384,128]{2,1,0:T(8,128)}, f32[12,384,128]{2,1,0:T(8,128)}) custom-call(s32[8]{0:T(128)} %place_cur.1, s32[8]{0:T(128)} %place_next.1, s32[1,256]{1,0:T(1,128)} %bitcast.19, s32[1,1024]{1,0:T(1,128)} %label_ref.1, f32[1,1024]{1,0:T(1,128)} %ref_ref.1, ...), custom_call_target="tpu_custom_call" | custom-call | flops 6039797760 | bytes 22544384 | tf_op jit(solution)/shard_map/pallas_call | solution.py:733
  143.9 7.4 %shard_map.148 = (bf16[256,512]{1,0:T(8,128)(2,1)}, f32[12,384,128]{2,1,0:T(8,128)}, f32[12,384,128]{2,1,0:T(8,128)}, f32[12,384,128]{2,1,0:T(8,128)}) custom-call(bf16[256,512]{1,0:T(8,128)(2,1)} %get-tuple-element.12.rows_ref, f32[12,384,128]{2,1,0:T(8,128)} %get-tuple-element.13.mast_in, f32[12,384,128]{2,1,0:T(8,128)} %get-tuple-element.14.mom1_in, ...), custom_call_target="tpu_custom_call" | custom-call | bytes 14155776 | tf_op jit(solution)/shard_map/pallas_call | solution.py:766

commit v3 on v2

--- a/solution.py
+++ b/solution.py
@@ -169,7 +169,7 @@
     mast_hbm,
     mom1_hbm,
     mom2_hbm,
-    out_ref,
+    out_hbm,
     nmast_hbm,
     nmom1_hbm,
     nmom2_hbm,
@@ -228,7 +228,7 @@
 ):
     me_s = lax.axis_index("slot")
     me_h = lax.axis_index("hid")
-    width = w_v.shape[2]
+    units, width = w_v.shape[1:]
     half = width // 2
     quarter = rows_in.shape[2]
     cap = rows_in.shape[1]
@@ -328,8 +328,9 @@
         at = pl.ds(pl.multiple_of(c * ROW_STEP, ROW_STEP), ROW_STEP)
         xc = x_v[at, :]
         rc = r_v[at, :]
-        gate = lax.dot_general(w_v[0], xc, ACROSS, preferred_element_type=F32)
-        up = lax.dot_general(w_v[1], xc, ACROSS, preferred_element_type=F32)
+        mixing_w = w_v[:2].reshape(2 * units, width)
+        both = lax.dot_general(mixing_w, xc, ACROSS, preferred_element_type=F32)
+        gate, up = both[:units], both[units:]
         turn = lax.dot_general(w_v[2], rc, ACROSS, preferred_element_type=F32)
         sig = jax.nn.sigmoid(gate)
         act = gate * sig
@@ -592,9 +593,11 @@
         ).wait_recv()
 
     loop(1, slots, ret_wait)
-    out_ref[...] = jnp.dot(
+    fwd_v[...] = jnp.dot(
         back_map[...], ret_recv[...].reshape(taken, quarter), preferred_element_type=F32
     ).astype(BF16)
+    out_store = pltpu.make_async_copy(fwd_v, out_hbm, load_sem.at[1])
+    out_store.start()
 
     def slot_sends(k):
         to = slot_peer(k)
@@ -615,34 +618,25 @@
     loop(0, slots, lambda s: lev2_copy(s).wait_send())
     for g in range(2):
         lev1_copy(g, 1 - pos).wait_send()
+    out_store.wait()
     for i, (_, dst, new) in enumerate(state):
         pltpu.make_async_copy(dst, new, store_sem.at[i]).wait()
 
 
-def results_kernel(rows_ref, mast_in, mom1_in, mom2_in, out_ref, mast_out, mom1_out, mom2_out, held, sem):
-    parts = sem.shape[2]
-    size = held.shape[1] // parts
-
-    src = (mast_in, mom1_in, mom2_in)
-    dst = (mast_out, mom1_out, mom2_out)
-
-    def come(i, c):
+def results_kernel(rows_in, mast_in, mom1_in, mom2_in, rows_out, mast_out, mom1_out, mom2_out, sem):
+    parts = sem.shape[1]
+    size = mast_in.shape[0] // parts
+    moves = [pltpu.make_async_copy(rows_in, rows_out, sem.at[3, 0])]
+    for c in range(parts):
         at = pl.ds(c * size, size)
-        return pltpu.make_async_copy(src[i].at[at], held.at[i, at], sem.at[0, i, c])
-
-    def go(i, c):
-        at = pl.ds(c * size, size)
-        return pltpu.make_async_copy(held.at[i, at], dst[i].at[at], sem.at[1, i, c])
-
-    every = [(i, c) for i in range(3) for c in range(parts)]
-    for i, c in every:
-        come(i, c).start()
-    out_ref[...] = rows_ref[...]
-    for i, c in every:
-        come(i, c).wait()
-        go(i, c).start()
-    for i, c in every:
-        go(i, c).wait()
+        for i, (src, dst) in enumerate(
+            ((mast_in, mast_out), (mom1_in, mom1_out), (mom2_in, mom2_out))
+        ):
+            moves.append(pltpu.make_async_copy(src.at[at], dst.at[at], sem.at[i, c]))
+    for move in moves:
+        move.start()
+    for move in moves:
+        move.wait()
 
 
 def fused_shards(
@@ -739,7 +733,7 @@
             state_shape,
         ),
         in_specs=[smem, smem, vmem, vmem, vmem] + [anywhere] * 7,
-        out_specs=(vmem, anywhere, anywhere, anywhere),
+        out_specs=(anywhere,) * 4,
         scratch_shapes=scratch,
         compiler_params=pltpu.CompilerParams(
             collective_id=0, has_side_effects=True, vmem_limit_bytes=VMEM_BYTES
@@ -771,10 +765,10 @@
             state_shape,
             state_shape,
         ),
-        in_specs=[vmem] + [anywhere] * 3,
-        out_specs=(vmem, anywhere, anywhere, anywhere),
-        scratch_shapes=[pltpu.VMEM((3,) + lines, F32), dma((2, 3, experts))],
-        compiler_params=pltpu.CompilerParams(vmem_limit_bytes=VMEM_BYTES),
+        in_specs=[anywhere] * 4,
+        out_specs=(anywhere,) * 4,
+        scratch_shapes=[dma((4, experts))],
+        compiler_params=pltpu.CompilerParams(vmem_limit_bytes=8 * 1024 * 1024),
         cost_estimate=pl.CostEstimate(
             flops=0, bytes_accessed=24 * master.size, transcendentals=0
         ),
@@ -783,7 +777,7 @@
     return (out_rows, new_master.reshape(shape), new_first.reshape(shape), new_second.reshape(shape))
 
 
-VMEM_BYTES = 60 * 1024 * 1024
+VMEM_BYTES = 46 * 1024 * 1024
 
 
 def step(*arrays):

time: 152 us -> 151 us (level)
  Pallas kernels: 151 us -> 145 us
  local copies, waits for them, and re-layouts: 0 us -> 4.3 us
    pallas_call x1, Pallas kernels: 7.43 us -> 3.11 us  [fused_shards(): pl.pallas_call(results_kernel, out_shape=(jax.ShapeDtypeStruct(fwd_rows.s...]
    unnamed x0 -> x12, local copies, waits for them, and re-layouts: none -> 4.3 us
where the time goes in v3:
time: 151 us; the launch traced here: 150 us
  Pallas kernels  145 us (96%)
  local copies, waits for them, and re-layouts  4.3 us (3%)
    pallas_call x1, Pallas kernels, fused_shards(): pl.pallas_call(functools.partial(kto_kernel, slots, hids, owned, experts)...  142 us
    unnamed x12, local copies, waits for them, and re-layouts  4.3 us
    pallas_call x1, Pallas kernels, fused_shards(): pl.pallas_call(results_kernel, out_shape=(jax.ShapeDtypeStruct(fwd_rows.s...  3.11 us

profile of v3, /device:TPU:1, one launch (start us, length us, event | category | flops | bytes accessed | tf_op | source)
XLA Modules:
  0.0 150.4 jit_solution(13399598501120617691)
XLA Ops:
  0.6 0.0 copy-start
  0.6 0.9 copy-done
  1.6 0.0 copy-start.1
  1.6 0.7 copy-done.1
  2.3 0.0 copy-start.2
  2.3 0.7 copy-done.2
  3.0 0.0 copy-start.3
  3.0 0.7 copy-done.3
  3.6 0.0 copy-start.4
  3.6 0.7 copy-done.4
  4.3 0.0 copy-start.5
  4.3 0.7 copy-done.5
  5.0 142.3 %shard_map.147 = (bf16[256,512]{1,0:T(8,128)(2,1)S(1)}, f32[12,384,128]{2,1,0:T(8,128)S(1)}, f32[12,384,128]{2,1,0:T(8,128)S(1)}, f32[12,384,128]{2,1,0:T(8,128)S(1)}) custom-call(s32[8]{0:T(128)S(1)} %copy-done.4, s32[8]{0:T(128)S(1)} %copy-done.5, s32[1,256]{1,0:T(1,128)S(1)} %bitcast.10, s32[1,1024]{1,0:T(1,128)S(1)} %copy-done.1, ...), custom_call_target="tpu_custom_call" | custom-call | flops 6039797760 | bytes 22544384 | tf_op jit(solution)/shard_map/pallas_call | solution.py:727
  147.3 3.1 %shard_map.148 = (bf16[256,512]{1,0:T(8,128)(2,1)}, f32[12,384,128]{2,1,0:T(8,128)}, f32[12,384,128]{2,1,0:T(8,128)}, f32[12,384,128]{2,1,0:T(8,128)}) custom-call(bf16[256,512]{1,0:T(8,128)(2,1)S(1)} %get-tuple-element.12.rows_in, f32[12,384,128]{2,1,0:T(8,128)S(1)} %get-tuple-element.13.mast_in, f32[12,384,128]{2,1,0:T(8,128)S(1)} %get-tuple-element.14.mom1_in, ...), custom_call_target="tpu_custom_call" | custom-call | bytes 14155776 | tf_op jit(solution)/shard_map/pallas_call | solution.py:760
Async XLA Ops:
  0.6 1.0 copy-start
  1.6 0.7 copy-start.1
  2.3 0.7 copy-start.2
  3.0 0.7 copy-start.3
  3.6 0.7 copy-start.4
  4.3 0.7 copy-start.5

commit v4 on v3

--- a/solution.py
+++ b/solution.py
@@ -157,11 +157,11 @@
     hids,
     owned,
     experts,
-    place_cur,
-    place_next,
-    route_ref,
-    label_ref,
-    ref_ref,
+    place_cur_hbm,
+    place_next_hbm,
+    route_hbm,
+    label_hbm,
+    ref_hbm,
     fwd_hbm,
     w_hbm,
     x_hbm,
@@ -173,6 +173,11 @@
     nmast_hbm,
     nmom1_hbm,
     nmom2_hbm,
+    place_cur,
+    place_next,
+    route_ref,
+    label_ref,
+    ref_ref,
     fwd_v,
     rows_in,
     back_map,
@@ -204,6 +209,7 @@
     ret_send,
     ret_recv,
     load_sem,
+    small_sem,
     xr_sem,
     mom_sem,
     store_sem,
@@ -239,8 +245,23 @@
     pieces = mixing + half // quarter
     steps = rows // ROW_STEP
 
+    def flipped(bits):
+        found, unit = 0, 1
+        while unit < slots:
+            bit = lax.rem(me_s // unit, 2)
+            found = found + unit * (1 - bit if bits // unit % 2 else bit)
+            unit *= 2
+        return found
+
+    across_middle = list(range(slots // 2, slots))
+    near = list(range(1, slots // 2))
+    turns = across_middle[:1]
+    for i, bits in enumerate(near):
+        turns += [bits, across_middle[i + 1]]
+    partners = [flipped(bits) for bits in turns] + [me_s]
+
     def slot_peer(k):
-        return lax.rem(me_s + k, slots)
+        return partners[k - 1]
 
     def hid_peer(k):
         return lax.rem(me_h + k, hids)
@@ -262,8 +283,26 @@
 
         lax.fori_loop(low, high, step, 0)
 
+    def each(low, high, body):
+        for k in range(low, high):
+            body(k)
+
     fwd_load = pltpu.make_async_copy(fwd_hbm, fwd_v, load_sem.at[1])
     fwd_load.start()
+    small = [
+        pltpu.make_async_copy(src, dst, small_sem.at[i])
+        for i, (src, dst) in enumerate(
+            (
+                (route_hbm, route_ref),
+                (label_hbm, label_ref),
+                (ref_hbm, ref_ref),
+                (place_cur_hbm, place_cur),
+                (place_next_hbm, place_next),
+            )
+        )
+    ]
+    for copy in small:
+        copy.start()
     w_load = pltpu.make_async_copy(w_hbm, w_v, load_sem.at[0])
     w_load.start()
 
@@ -291,9 +330,11 @@
     def greet_hid(k):
         pl.semaphore_signal(barrier, inc=1, device_id=(me_s, hid_peer(k)), device_id_type=MESH)
 
-    loop(1, slots, greet_slot)
+    each(1, slots, greet_slot)
     loop(1, hids, greet_hid)
 
+    for copy in small:
+        copy.wait()
     count = fwd_v.shape[0]
     named = jnp.broadcast_to(route_ref[...].astype(F32), (count, count))
     first = lax.broadcasted_iota(jnp.int32, (count, count), 0)
@@ -317,7 +358,7 @@
             rows_in.at[to], rows_full.at[me_h, me_s], row_ss.at[to], row_rs.at[me_s], slot=to
         )
 
-    loop(1, slots, lambda k: row_copy(slot_peer(k)).start())
+    each(1, slots, lambda k: row_copy(slot_peer(k)).start())
     rows_full[me_h, me_s] = rows_in[me_s]
 
     w_load.wait()
@@ -362,14 +403,14 @@
     def tot_copy(to):
         return remote(tot_v, tot_all.at[me_s], tot_ss.at[to], tot_rs.at[me_s], slot=to)
 
-    loop(1, slots, lambda k: tot_copy(slot_peer(k)).start())
+    each(1, slots, lambda k: tot_copy(slot_peer(k)).start())
     tot_all[me_s] = tot_v[...]
 
     def tot_wait(k):
         frm = slot_peer(k)
         remote(tot_v, tot_all.at[frm], tot_ss.at[frm], tot_rs.at[frm], slot=frm).wait_recv()
 
-    loop(1, slots, tot_wait)
+    each(1, slots, tot_wait)
     total = tot_all[0]
     for s in range(1, slots):
         total = total + tot_all[s]
@@ -388,7 +429,7 @@
         )
 
     def send_grads(p):
-        loop(1, slots, lambda k: grad_copy(p, slot_peer(k)).start())
+        each(1, slots, lambda k: grad_copy(p, slot_peer(k)).start())
         grecv[p, me_s] = gsend[p, me_s]
 
     def mixing_grads(p):
@@ -418,7 +459,7 @@
             rows_in.at[frm], rows_full.at[me_h, frm], row_ss.at[frm], row_rs.at[frm], slot=frm
         ).wait_recv()
 
-    loop(1, slots, row_wait)
+    each(1, slots, row_wait)
 
     def gather_copy(to):
         return remote(
@@ -448,7 +489,7 @@
                 gsend.at[p, frm], grecv.at[p, frm], g_ss.at[p, frm], g_rs.at[p, frm], slot=frm
             ).wait_recv()
 
-        loop(1, slots, grad_wait)
+        each(1, slots, grad_wait)
 
         def lane_block(j):
             lanes = pl.ds(pl.multiple_of(j * 128, 128), 128)
@@ -480,7 +521,7 @@
                 wsend[p, t, :, lanes] = chosen.astype(BF16)
 
         loop(0, part_blocks, lane_block)
-        loop(1, slots, lambda k: weight_copy(p, slot_peer(k)).start())
+        each(1, slots, lambda k: weight_copy(p, slot_peer(k)).start())
         wrecv[p, me_s] = wsend[p, me_s]
 
     def mixing_adam(p):
@@ -510,7 +551,7 @@
                 wsend.at[p, frm], wrecv.at[p, frm], w_ss.at[p, frm], w_rs.at[p, frm], slot=frm
             ).wait_recv()
 
-        loop(1, slots, one)
+        each(1, slots, one)
 
     mixed = None
     for h in range(hids):
@@ -581,9 +622,9 @@
         @pl.when(pos == turn)
         def _(turn=turn):
             lev1_copy(1 - grp, turn).wait_recv()
-            loop(1, slots + 1, to_far)
+            each(1, slots + 1, to_far)
             lev1_copy(grp, turn).wait_recv()
-            loop(1, slots, give_back)
+            each(1, slots, give_back)
             ret_recv[me_s] = last_sum(me_s)
 
     def ret_wait(k):
@@ -592,7 +633,7 @@
             ret_send.at[frm], ret_recv.at[frm], ret_ss.at[frm], ret_rs.at[frm], slot=frm
         ).wait_recv()
 
-    loop(1, slots, ret_wait)
+    each(1, slots, ret_wait)
     fwd_v[...] = jnp.dot(
         back_map[...], ret_recv[...].reshape(taken, quarter), preferred_element_type=F32
     ).astype(BF16)
@@ -613,7 +654,7 @@
         part_copy(to).wait_send()
         gather_copy(to).wait_send()
 
-    loop(1, slots, slot_sends)
+    each(1, slots, slot_sends)
     loop(1, hids, hid_sends)
     loop(0, slots, lambda s: lev2_copy(s).wait_send())
     for g in range(2):
@@ -664,12 +705,16 @@
     cap = 2 * fwd_rows.shape[0] // slots
     taken = slots * cap
     lines = (experts * kinds, owned * width // 128, 128)
-    vmem = pl.BlockSpec(memory_space=pltpu.VMEM)
-    smem = pl.BlockSpec(memory_space=pltpu.SMEM)
+    pinned = pl.BlockSpec(memory_space=pltpu.HBM)
     anywhere = pl.BlockSpec(memory_space=pl.ANY)
     pieces = (width // quarter + half // quarter, slots, 2 * owned, quarter)
     dma = pltpu.SemaphoreType.DMA
     scratch = [
+        pltpu.SMEM(place_cur.shape, jnp.int32),
+        pltpu.SMEM(place_next.shape, jnp.int32),
+        pltpu.VMEM((1, fwd_rows.shape[0]), jnp.int32),
+        pltpu.VMEM(labels.shape, jnp.int32),
+        pltpu.VMEM(ref_logratio.shape, F32),
         pltpu.VMEM(fwd_rows.shape, BF16),
         pltpu.VMEM((slots, cap, quarter), BF16),
         pltpu.VMEM((fwd_rows.shape[0], taken), BF16),
@@ -701,6 +746,7 @@
         pltpu.VMEM((slots, cap, quarter), BF16),
         pltpu.VMEM((slots, cap, quarter), BF16),
         dma((2,)),
+        dma((5,)),
         dma((2, rows // ROW_STEP)),
         dma((3,)),
         dma((3,)),
@@ -732,7 +778,7 @@
             state_shape,
             state_shape,
         ),
-        in_specs=[smem, smem, vmem, vmem, vmem] + [anywhere] * 7,
+        in_specs=[pinned] * 12,
         out_specs=(anywhere,) * 4,
         scratch_shapes=scratch,
         compiler_params=pltpu.CompilerParams(
@@ -768,7 +814,7 @@
         in_specs=[anywhere] * 4,
         out_specs=(anywhere,) * 4,
         scratch_shapes=[dma((4, experts))],
-        compiler_params=pltpu.CompilerParams(vmem_limit_bytes=8 * 1024 * 1024),
+        compiler_params=pltpu.CompilerParams(vmem_limit_bytes=VMEM_BYTES),
         cost_estimate=pl.CostEstimate(
             flops=0, bytes_accessed=24 * master.size, transcendentals=0
         ),
@@ -777,7 +823,7 @@
     return (out_rows, new_master.reshape(shape), new_first.reshape(shape), new_second.reshape(shape))
 
 
-VMEM_BYTES = 46 * 1024 * 1024
+VMEM_BYTES = 60 * 1024 * 1024
 
 
 def step(*arrays):
@@ -786,6 +832,7 @@
     owned = weights.shape[2] // slots
     cap = 2 * fwd_rows.shape[0] // slots
     fits = owned % 8 == 0 and cap % 16 == 0 and lax.axis_size("hid") == 4
+    fits = fits and slots & (slots - 1) == 0
     fits = fits and weights.shape[3] == 4 * fwd_rows.shape[1] and weights.shape[3] % 1024 == 0
     fits = fits and arrays[4].shape[1] % ROW_STEP == 0
     return (fused_shards if fits else shards)(*arrays)

time: 151 us -> 368 us (2.44)
  Pallas kernels: 145 us -> 367 us
  local copies, waits for them, and re-layouts: 4.3 us -> 0 us
    pallas_call x1, Pallas kernels: 3.11 us -> 224 us  [fused_shards(): pl.pallas_call(results_kernel, out_shape=(jax.ShapeDtypeStruct(fwd_rows.s...]
    unnamed x12 -> x0, local copies, waits for them, and re-layouts: 4.3 us -> none
where the time goes in v4:
time: 368 us
  Pallas kernels  367 us (100%)
    pallas_call x1, Pallas kernels, fused_shards(): pl.pallas_call(results_kernel, out_shape=(jax.ShapeDtypeStruct(fwd_rows.s...  224 us
    pallas_call x1, Pallas kernels, fused_shards(): pl.pallas_call(functools.partial(kto_kernel, slots, hids, owned, experts)...  143 us

profile of v4, /device:TPU:1, one launch (start us, length us, event | category | flops | bytes accessed | tf_op | source)
XLA Modules:
  0.0 367.7 jit_solution(6614898427945894087)
XLA Ops:
  0.6 143.4 %shard_map.147 = (bf16[256,512]{1,0:T(8,128)(2,1)}, f32[12,384,128]{2,1,0:T(8,128)}, f32[12,384,128]{2,1,0:T(8,128)}, f32[12,384,128]{2,1,0:T(8,128)}) custom-call(s32[8]{0:T(128)} %place_cur_hbm.1, s32[8]{0:T(128)} %place_next_hbm.1, s32[1,256]{1,0:T(1,128)} %bitcast.19, s32[1,1024]{1,0:T(1,128)} %label_hbm.1, f32[1,1024]{1,0:T(1,128)} %ref_hbm.1, ...), custom_call_target="tpu_custom_call" | custom-call | flops 6039797760 | bytes 22544384 | tf_op jit(solution)/shard_map/pallas_call | solution.py:773
  144.1 223.6 %shard_map.148 = (bf16[256,512]{1,0:T(8,128)(2,1)}, f32[12,384,128]{2,1,0:T(8,128)}, f32[12,384,128]{2,1,0:T(8,128)}, f32[12,384,128]{2,1,0:T(8,128)}) custom-call(bf16[256,512]{1,0:T(8,128)(2,1)} %get-tuple-element.12.rows_in, f32[12,384,128]{2,1,0:T(8,128)} %get-tuple-element.13.mast_in, f32[12,384,128]{2,1,0:T(8,128)} %get-tuple-element.14.mom1_in, ...), custom_call_target="tpu_custom_call" | custom-call | bytes 14155776 | tf_op jit(solution)/shard_map/pallas_call | solution.py:806

commit v5 on v3

--- a/solution.py
+++ b/solution.py
@@ -157,10 +157,7 @@
     hids,
     owned,
     experts,
-    place_cur,
-    place_next,
-    route_ref,
-    label_ref,
+    ints_ref,
     ref_ref,
     fwd_hbm,
     w_hbm,
@@ -173,6 +170,7 @@
     nmast_hbm,
     nmom1_hbm,
     nmom2_hbm,
+    ints,
     fwd_v,
     rows_in,
     back_map,
@@ -204,6 +202,7 @@
     ret_send,
     ret_recv,
     load_sem,
+    ints_sem,
     xr_sem,
     mom_sem,
     store_sem,
@@ -264,6 +263,8 @@
 
     fwd_load = pltpu.make_async_copy(fwd_hbm, fwd_v, load_sem.at[1])
     fwd_load.start()
+    ints_load = pltpu.make_async_copy(ints_ref, ints, ints_sem.at[0])
+    ints_load.start()
     w_load = pltpu.make_async_copy(w_hbm, w_v, load_sem.at[0])
     w_load.start()
 
@@ -295,7 +296,8 @@
     loop(1, hids, greet_hid)
 
     count = fwd_v.shape[0]
-    named = jnp.broadcast_to(route_ref[...].astype(F32), (count, count))
+    targets = ints_ref[:, rows : rows + count].astype(F32)
+    named = jnp.broadcast_to(targets, (count, count))
     first = lax.broadcasted_iota(jnp.int32, (count, count), 0)
     second = lax.broadcasted_iota(jnp.int32, (count, count), 1)
     before = (named == jnp.transpose(named)) & (first < second)
@@ -374,7 +376,7 @@
     for s in range(1, slots):
         total = total + tot_all[s]
     center = total[:, :1] * (1.0 / (slots * rows))
-    slope = kto_slope(scores, label_ref[...], center)
+    slope = kto_slope(scores, ints_ref[:, :rows], center)
 
     for s in range(slots):
         units = pl.ds(s * owned, owned)
@@ -429,8 +431,10 @@
 
     for i, (src, dst, _) in enumerate(state):
         pltpu.make_async_copy(src, dst, mom_sem.at[i]).wait()
-    cur = [place_cur[s] for s in range(slots)]
-    nxt = [place_next[s] for s in range(slots)]
+    ints_load.wait()
+    places = rows + count
+    cur = [ints[0, places + s] for s in range(slots)]
+    nxt = [ints[0, places + slots + s] for s in range(slots)]
     is_cur = [[jnp.where(cur[s] == e, 1.0, 0.0) for s in range(slots)] for e in range(experts)]
     is_nxt = [[jnp.where(nxt[t] == e, 1.0, 0.0) for t in range(slots)] for e in range(experts)]
     blocks = width // 128
@@ -663,13 +667,16 @@
     quarter = fwd_rows.shape[1]
     cap = 2 * fwd_rows.shape[0] // slots
     taken = slots * cap
+    ints = jnp.concatenate(
+        [labels, routes.reshape(1, -1), place_cur[None], place_next[None]], axis=1
+    )
     lines = (experts * kinds, owned * width // 128, 128)
     vmem = pl.BlockSpec(memory_space=pltpu.VMEM)
-    smem = pl.BlockSpec(memory_space=pltpu.SMEM)
     anywhere = pl.BlockSpec(memory_space=pl.ANY)
     pieces = (width // quarter + half // quarter, slots, 2 * owned, quarter)
     dma = pltpu.SemaphoreType.DMA
     scratch = [
+        pltpu.SMEM(ints.shape, jnp.int32),
         pltpu.VMEM(fwd_rows.shape, BF16),
         pltpu.VMEM((slots, cap, quarter), BF16),
         pltpu.VMEM((fwd_rows.shape[0], taken), BF16),
@@ -701,6 +708,7 @@
         pltpu.VMEM((slots, cap, quarter), BF16),
         pltpu.VMEM((slots, cap, quarter), BF16),
         dma((2,)),
+        dma((1,)),
         dma((2, rows // ROW_STEP)),
         dma((3,)),
         dma((3,)),
@@ -732,7 +740,7 @@
             state_shape,
             state_shape,
         ),
-        in_specs=[smem, smem, vmem, vmem, vmem] + [anywhere] * 7,
+        in_specs=[vmem, vmem] + [anywhere] * 7,
         out_specs=(anywhere,) * 4,
         scratch_shapes=scratch,
         compiler_params=pltpu.CompilerParams(
@@ -744,10 +752,7 @@
             transcendentals=2 * rows * units,
         ),
     )(
-        place_cur,
-        place_next,
-        routes.reshape(1, fwd_rows.shape[0]),
-        labels,
+        ints,
         ref_logratio,
         fwd_rows,
         slot_weights[0],

time: 151 us -> 148 us (0.980)
  local copies, waits for them, and re-layouts: 4.3 us -> 2.43 us
    unnamed x12 -> x4, local copies, waits for them, and re-layouts: 4.3 us -> 1.64 us
where the time goes in v5:
time: 148 us
  Pallas kernels  145 us (98%)
  local copies, waits for them, and re-layouts  2.43 us (2%)
    pallas_call x1, Pallas kernels, fused_shards(): pl.pallas_call(functools.partial(kto_kernel, slots, hids, owned, experts)...  142 us
    pallas_call x1, Pallas kernels, fused_shards(): pl.pallas_call(results_kernel, out_shape=(jax.ShapeDtypeStruct(fwd_rows.s...  3.11 us

profile of v5, /device:TPU:1, one launch (start us, length us, event | category | flops | bytes accessed | tf_op | source)
XLA Modules:
  0.0 147.9 jit_solution(11137511036734060335)
XLA Ops:
  0.6 0.8 concatenate.3.ints_ref
  1.4 0.0 copy-start
  1.4 0.9 copy-done
  2.4 0.0 copy-start.1
  2.4 0.7 copy-done.1
  3.1 141.7 %shard_map.147 = (bf16[256,512]{1,0:T(8,128)(2,1)S(1)}, f32[12,384,128]{2,1,0:T(8,128)S(1)}, f32[12,384,128]{2,1,0:T(8,128)S(1)}, f32[12,384,128]{2,1,0:T(8,128)S(1)}) custom-call(s32[1,1296]{1,0:T(1,128)S(1)} %concatenate.3.ints_ref, f32[1,1024]{1,0:T(1,128)S(1)} %copy-done.1, bf16[256,512]{1,0:T(8,128)(2,1)S(1)} %copy-done, ...), custom_call_target="tpu_custom_call" | custom-call | flops 6039797760 | bytes 22544384 | tf_op jit(solution)/shard_map/pallas_call | solution.py:735
  144.8 3.1 %shard_map.148 = (bf16[256,512]{1,0:T(8,128)(2,1)}, f32[12,384,128]{2,1,0:T(8,128)}, f32[12,384,128]{2,1,0:T(8,128)}, f32[12,384,128]{2,1,0:T(8,128)}) custom-call(bf16[256,512]{1,0:T(8,128)(2,1)S(1)} %get-tuple-element.12.rows_in, f32[12,384,128]{2,1,0:T(8,128)S(1)} %get-tuple-element.13.mast_in, f32[12,384,128]{2,1,0:T(8,128)S(1)} %get-tuple-element.14.mom1_in, ...), custom_call_target="tpu_custom_call" | custom-call | bytes 14155776 | tf_op jit(solution)/shard_map/pallas_call | solution.py:765
Async XLA Ops:
  1.4 1.0 copy-start
  2.4 0.7 copy-start.1
